TPU v7x, 256 devices: a whole 4x4x8 slice. The times are simulated.
256 devices in a mesh: group: 8 (over z), member: 32 (over x, y, core).
Axes of the slice: x: 4, y: 4, z: 8, core: 2. Of those that a mesh axis runs over, the one named last changes fastest.
Arguments:
- hot_table: float32 [768, 1024], replicated, may hold values from -2.4 to 2.4
- hot_state: float32 [768], replicated, may hold values from 0.1 to 10
- cold_table: float32 [16384, 1024], P('member'), may hold values from -2.4 to 2.4
- cold_state: float32 [16384], P('member'), may hold values from 0.1 to 10
- relation_table: float32 [128, 1024], replicated, may hold values from -2.4 to 2.4
- relation_state: float32 [128], replicated, may hold values from 0.1 to 10
- cold_requests: int32 [256, 1024], P(('group', 'member')), may hold values from 0 to 512, as said below
- head_slots: int32 [262144], P(('group', 'member')), may hold values from 0 to 1791, as said below
- relation_index: int32 [262144], P(('group', 'member')), may hold values from 0 to 127
- tail_slots: int32 [262144], P(('group', 'member')), may hold values from 0 to 1791, as said below
- negative_slots: int32 [256, 512], P(('group', 'member')), may hold values from 0 to 1791, as said below
Outputs:
- new_hot_table: float32 [768, 1024], replicated
- new_hot_state: float32 [768], replicated
- new_cold_table: float32 [16384, 1024], P('member')
- new_cold_state: float32 [16384], P('member')
- new_relation_table: float32 [128, 1024], replicated
- new_relation_state: float32 [128], replicated
- mean_loss: float32 [], replicated
Inputs may be any that keep to these rules, and one draw needn't show every extreme that they name: `cold_requests`: entries o * 32 onward of a device's row name distinct rows of owner o's block; live entries come first and the rest hold 512; on every device some owner's 32 slots are all live, and one owner's slots are all live on every device. `head_slots`: an entry below 768 is a hot row; else entry - 768 = o * 32 + k is a live slot k of owner o in the list of the device that holds the triple. `tail_slots`: as head_slots. `negative_slots`: as head_slots, for the device that holds the block.
All inputs are finite; a program needn't handle non-finite values.
Results may differ from a plain program's by a relative error of at most 0.0055.
Values may be sent and summed in bfloat16 or wider, within the bound.
No kernel may reach another device: no remote copies, remote signals or barrier semaphores. Data moves between devices by JAX's collectives and lax.ppermute only.
A program may use at most 128 MiB of HBM per device.

v0:
```python
import jax
import jax.numpy as jnp
from jax import lax
from jax.sharding import PartitionSpec as P

learn_rate = 0.1


def complex_query(head_rows, relation_rows):
    half_width = head_rows.shape[-1] // 2
    head_real, head_imag = (head_rows[:, :half_width], head_rows[:, half_width:])
    relation_real, relation_imag = (relation_rows[:, :half_width], relation_rows[:, half_width:])
    return jnp.concatenate(
        [
            head_real * relation_real - head_imag * relation_imag,
            head_real * relation_imag + head_imag * relation_real,
        ],
        -1,
    )


def query_grads(query_grad, head_rows, relation_rows):
    half_width = head_rows.shape[-1] // 2
    head_real, head_imag = (head_rows[:, :half_width], head_rows[:, half_width:])
    relation_real, relation_imag = (relation_rows[:, :half_width], relation_rows[:, half_width:])
    grad_real, grad_imag = (query_grad[:, :half_width], query_grad[:, half_width:])
    head_grad = jnp.concatenate(
        [
            grad_real * relation_real + grad_imag * relation_imag,
            grad_imag * relation_real - grad_real * relation_imag,
        ],
        -1,
    )
    relation_grad = jnp.concatenate(
        [
            grad_real * head_real + grad_imag * head_imag,
            grad_imag * head_real - grad_real * head_imag,
        ],
        -1,
    )
    return (head_grad, relation_grad)


def device_terms(
    entity_rows, relation_half, head_slots, relation_index, tail_slots, negative_slots
):
    stretches, neg_count = negative_slots.shape
    row_width = entity_rows.shape[1]
    head_rows = jnp.take(entity_rows, head_slots, axis=0).astype(jnp.float32)
    tail_rows = jnp.take(entity_rows, tail_slots, axis=0).astype(jnp.float32)
    relation_rows = jnp.take(relation_half, relation_index, axis=0).astype(jnp.float32)
    negatives = jnp.take(entity_rows, negative_slots, axis=0)
    queries = complex_query(head_rows, relation_rows)
    positive = jnp.sum(queries * tail_rows, -1)
    blocks = queries.astype(jnp.bfloat16).reshape(stretches, -1, row_width)
    scores = jnp.einsum("cid,cjd->cij", blocks, negatives, preferred_element_type=jnp.float32)
    loss_sum = jnp.sum(jax.nn.softplus(-positive)) + jnp.sum(jax.nn.softplus(scores)) / neg_count
    pos_grad = jax.nn.sigmoid(positive) - 1.0
    score_grad = (jax.nn.sigmoid(scores) / neg_count).astype(jnp.bfloat16)
    query_grad = pos_grad[:, None] * tail_rows + jnp.einsum(
        "cij,cjd->cid", score_grad, negatives, preferred_element_type=jnp.float32
    ).reshape(-1, row_width)
    tail_grad = pos_grad[:, None] * queries
    negative_grad = jnp.einsum(
        "cij,cid->cjd", score_grad, blocks, preferred_element_type=jnp.float32
    ).reshape(-1, row_width)
    head_grad, relation_grad = query_grads(query_grad, head_rows, relation_rows)
    entity_grad = jnp.zeros((entity_rows.shape[0], row_width), jnp.float32)
    entity_grad = entity_grad.at[head_slots].add(head_grad)
    entity_grad = entity_grad.at[tail_slots].add(tail_grad)
    entity_grad = entity_grad.at[negative_slots.reshape(-1)].add(negative_grad)
    relation_total = jax.ops.segment_sum(
        relation_grad, relation_index, num_segments=relation_half.shape[0]
    )
    return (loss_sum, entity_grad, relation_total)


def adagrad(emb_table, acc_state, row_grad):
    new_state = acc_state + jnp.mean(row_grad * row_grad, -1)
    return (emb_table - learn_rate * row_grad / jnp.sqrt(new_state)[:, None], new_state)


def per_device(
    hot_table,
    hot_state,
    cold_table,
    cold_state,
    relation_table,
    relation_state,
    cold_requests,
    head_slots,
    relation_index,
    tail_slots,
    negative_slots,
):
    members = lax.axis_size("member")
    row_width = hot_table.shape[1]
    hot_count = hot_table.shape[0]
    owned_rows = cold_table.shape[0]
    wanted = cold_requests.reshape(members, -1)
    shard_half = cold_table.astype(jnp.bfloat16)
    received = lax.all_to_all(wanted, "member", split_axis=0, concat_axis=0, tiled=True)
    served = jnp.take(shard_half, received, axis=0, mode="fill", fill_value=0)
    returned = lax.all_to_all(served, "member", split_axis=0, concat_axis=0, tiled=True)
    entity_rows = jnp.concatenate([hot_table.astype(jnp.bfloat16), returned.reshape(-1, row_width)])
    relation_half = relation_table.astype(jnp.bfloat16)
    loss_sum, entity_grad, relation_grad = device_terms(
        entity_rows, relation_half, head_slots, relation_index, tail_slots, negative_slots
    )
    slot_grads = entity_grad[hot_count:].reshape(members, -1, row_width)
    arrived = lax.all_to_all(
        slot_grads.astype(jnp.bfloat16), "member", split_axis=0, concat_axis=0, tiled=True
    ).astype(slot_grads.dtype)
    owner_grad = jax.ops.segment_sum(
        arrived.reshape(-1, row_width), received.reshape(-1), num_segments=owned_rows
    )
    cold_total = lax.psum(owner_grad.astype(jnp.bfloat16), "group").astype(jnp.float32)
    new_cold_table, new_cold_state = adagrad(cold_table, cold_state, cold_total)
    hot_grad = entity_grad[:hot_count]
    batch_total = head_slots.shape[0] * lax.axis_size("group") * members
    hot_total, relation_total, total_loss = lax.psum(
        (hot_grad, relation_grad, loss_sum), ("group", "member")
    )
    new_hot_table, new_hot_state = adagrad(hot_table, hot_state, hot_total)
    new_relation_table, new_relation_state = adagrad(relation_table, relation_state, relation_total)
    mean_loss = total_loss / batch_total
    return (
        new_hot_table,
        new_hot_state,
        new_cold_table,
        new_cold_state,
        new_relation_table,
        new_relation_state,
        mean_loss,
    )


def solution(mesh):
    placed = (
        P(),
        P(),
        P("member", None),
        P("member"),
        P(),
        P(),
        P(("group", "member"), None),
        P(("group", "member")),
        P(("group", "member")),
        P(("group", "member")),
        P(("group", "member"), None),
    )
    return jax.shard_map(
        per_device,
        mesh=mesh,
        in_specs=placed,
        out_specs=(P(), P(), P("member", None), P("member"), P(), P(), P()),
        check_vma=False,
    )
```

profile of v0, /device:TPU:2, one launch (start us, length us, event | category | flops | bytes accessed | tf_op | source)
XLA Modules:
  0.0 588.6 jit_solution(14123661488598881230)
XLA Ops:
  8.5 1.3 reduce.10
  10.6 7.6 %all-to-all-start = ((s32[32,1,32]{2,1,0:T(1,128)}), s32[32,1,32]{2,1,0:T(1,128)S(1)}, u32[]{:S(2)}, u32[]{:S(2)}) async-start(s32[32,1,32]{2,1,0:T(1,128)} %all_to_all.16), calls=%async_computation | async-start | bytes 32768 | tf_op jit(solution)/shard_map/all_to_all | solution.py:102
  18.2 1.8 convert_element_type.40
  19.9 4.3 all-to-all-done
  24.4 4.1 gather_fusion
  28.5 1.5 broadcast_select_fusion.1
  30.0 6.1 %all-to-all-start.1 = ((bf16[32,32,1024]{2,1,0:T(8,128)(2,1)}), bf16[32,32,1024]{2,1,0:T(8,128)(2,1)}, u32[]{:S(2)}, u32[]{:S(2)}) async-start(bf16[32,32,1024]{2,1,0:T(8,128)(2,1)} %broadcast_select_fusion.1), calls=%async_computation.1 | async-start | bytes 4194304 | tf_op jit(solution)/shard_map/all_to_all | solution.py:104
  36.1 1.1 convert_element_type.42
  37.2 1.4 convert_element_type.39
  38.7 5.3 gather_fusion.1
  44.0 4.0 copy.28
  48.2 13.9 %all-to-all-done.1 = bf16[32,32,1024]{2,1,0:T(8,128)(2,1)} async-done(((bf16[32,32,1024]{2,1,0:T(8,128)(2,1)}), bf16[32,32,1024]{2,1,0:T(8,128)(2,1)}, u32[]{:S(2)}, u32[]{:S(2)}) %all-to-all-start.1) | async-done | bytes 2097184 | tf_op jit(solution)/shard_map/all_to_all | solution.py:104
  62.1 4.3 pad_maximum_fusion.3
  66.3 6.0 %gather_fusion.2 = bf16[512,1024]{1,0:T(8,128)(2,1)} fusion(bf16[1792,1024]{1,0:T(8,128)(2,1)} %pad_maximum_fusion.3, s32[1024]{0:T(1024)S(1)} %pad_clamp_fusion), kind=kCustom, calls=%fused_computation.4 | custom fusion | bytes 2099200 | tf_op jit(solution)/shard_map/jit(_take)/gather | solution.py:52
  72.3 8.5 %gather_fusion.4 = bf16[1024,1024]{1,0:T(8,128)(2,1)} fusion(bf16[1792,1024]{1,0:T(8,128)(2,1)} %pad_maximum_fusion.3, s32[1024]{0:T(1024)S(1)} %get-tuple-element.29), kind=kCustom, calls=%fused_computation.1.clone | custom fusion | bytes 4198400 | tf_op jit(solution)/shard_map/jit(_take)/gather | solution.py:50
  80.8 8.5 %gather_fusion.3 = bf16[1024,1024]{1,0:T(8,128)(2,1)} fusion(bf16[1792,1024]{1,0:T(8,128)(2,1)} %pad_maximum_fusion.3, s32[1024]{0:T(1024)S(1)} %get-tuple-element.30), kind=kCustom, calls=%fused_computation.clone | custom fusion | bytes 4198400 | tf_op jit(solution)/shard_map/jit(_take)/gather | solution.py:49
  89.4 4.0 copy.29
  93.3 4.4 copy.27
  97.7 2.8 select_convert_fusion
  100.5 1.0 multiply_subtract_fusion.2
  103.6 2.9 fusion.11
  106.5 2.7 fusion.14
  109.3 3.6 fusion.1
  112.9 2.4 fusion.6
  115.3 6.7 %multiply_add_fusion = (f32[1024,512]{0,1:T(8,128)S(1)}, f32[1024,512]{0,1:T(8,128)}, f32[1024,512]{0,1:T(8,128)}, f32[1024,512]{0,1:T(8,128)}) fusion(f32[1024,1024]{0,1:T(8,128)} %fusion.1, f32[1024,1024]{0,1:T(8,128)S(1)} %get-tuple-element.34, f32[1024,1024]{0,1:T(8,128)S(1)} %get-tuple-element.35), kind=kLoop, calls=%fused_computation.36 | loop fusion | flops 6291456 | bytes 20971520 | tf_op jit(solution)/shard_map/add | solution.py:36
  122.0 4.1 pad_maximum_fusion.2
  126.1 5.4 copy.32
  131.5 5.6 copy.31
  137.1 4.8 pad_maximum_fusion.1
  141.9 5.4 copy.30
  147.2 11.1 %scatter_custom_fusion.4 = f32[128,1024]{1,0:T(8,128)} fusion(s32[1024]{0:T(1024)S(1)} %copy-done.5, f32[1024,1024]{1,0:T(8,128)} %copy.32, f32[]{:T(128)} %constant.43.clone.1), kind=kCustom, calls=%fused_computation.51 | custom fusion | flops 1048576 | bytes 524800 | tf_op jit(solution)/shard_map/scatter-add | solution.py:72
  158.3 13.7 %scatter_custom_fusion = f32[1792,1024]{1,0:T(8,128)} fusion(s32[1024]{0:T(1024)S(1)} %get-tuple-element.31, f32[1024,1024]{1,0:T(8,128)} %copy.30, f32[]{:T(128)} %constant.43.clone.1), kind=kCustom, calls=%fused_computation.22 | custom fusion | flops 1048576 | bytes 7340544 | tf_op jit(solution)/shard_map/scatter-add | solution.py:69
  172.0 16.3 %scatter_fusion = f32[1792,1024]{1,0:T(8,128)} fusion(f32[1792,1024]{1,0:T(8,128)} %scatter_custom_fusion, s32[1024]{0:T(1024)S(1)} %get-tuple-element.28, f32[1024,1024]{1,0:T(8,128)} %copy.31), kind=kCustom, calls=%fused_computation.6 | custom fusion | flops 1048576 | bytes 12587008 | tf_op jit(solution)/shard_map/scatter-add | solution.py:70
  188.4 11.9 %scatter_fusion.1 = f32[1792,1024]{1,0:T(8,128)} fusion(f32[1792,1024]{1,0:T(8,128)} %scatter_fusion, s32[512]{0:T(512)S(1)} %bitcast.17, f32[512,1024]{1,0:T(8,128)} %fusion.14), kind=kCustom, calls=%fused_computation.7 | custom fusion | flops 524288 | bytes 6293504 | tf_op jit(solution)/shard_map/scatter-add | solution.py:71
  200.3 4.0 slice.53
  204.3 3.8 slice.80
  208.1 7.6 %all-to-all-start.2 = ((bf16[32,32,1024]{2,1,0:T(8,128)(2,1)}), bf16[32,32,1024]{2,1,0:T(8,128)(2,1)}, u32[]{:S(2)}, u32[]{:S(2)}) async-start(bf16[32,32,1024]{2,1,0:T(8,128)(2,1)} %bitcast.13), calls=%async_computation.2 | async-start | bytes 4194304 | tf_op jit(solution)/shard_map/all_to_all | solution.py:111
  217.9 94.8 %psum.31 = f32[]{:T(128)} all-reduce(f32[]{:T(128)S(6)} %add.152), channel_id=1, replica_groups=mesh['group'=8,'member'=32] {'group','member'}, use_global_device_ids=true, to_apply=%region_14.16 | all-reduce | flops 1 | bytes 8 | tf_op jit(solution)/shard_map/psum | solution.py:121
  313.4 168.5 %all-reduce.6.cloned.1.call-done = (f32[768,1024]{1,0:T(8,128)}, f32[128,1024]{1,0:T(8,128)}) async-done(((f32[768,1024]{1,0:T(8,128)}, f32[128,1024]{1,0:T(8,128)}), (f32[768,1024]{1,0:T(8,128)}, f32[128,1024]{1,0:T(8,128)})) %all-reduce.6.cloned.1.call-update) | async-done | bytes 3670032 | tf_op jit(solution)/shard_map/psum | solution.py:121
  481.9 1.2 multiply_reduce_fusion.1
  483.1 2.2 multiply_reduce_fusion
  485.9 11.1 %scatter_custom_fusion.3 = f32[512,1024]{1,0:T(8,128)} fusion(s32[1024]{0:T(1024)S(1)} %reshape.261, bf16[1024,1024]{1,0:T(8,128)(2,1)} %bitcast.9, f32[]{:T(128)} %constant.43.clone.1), kind=kCustom, calls=%fused_computation.19 | custom fusion | flops 2097152 | bytes 4194308 | tf_op jit(solution)/shard_map/scatter-add | solution.py:114
  496.9 2.7 convert_element_type.48
  500.2 2.1 divide_subtract_fusion.1
  502.3 4.3 divide_subtract_fusion
  506.7 67.4 %all-reduce.4.cloned.1.call-done = bf16[512,1024]{1,0:T(8,128)(2,1)} async-done(((bf16[512,1024]{1,0:T(8,128)(2,1)}), bf16[512,1024]{1,0:T(8,128)(2,1)}) %all-reduce.4.cloned.1.call-update) | async-done | bytes 1048592 | tf_op jit(solution)/shard_map/psum | solution.py:117
  574.1 1.5 fusion.10
  576.2 3.7 fusion.9
  (47 shorter events, 6.1 us)
Async XLA Ops:
  10.6 13.7 %all-to-all-start = ((s32[32,1,32]{2,1,0:T(1,128)}), s32[32,1,32]{2,1,0:T(1,128)S(1)}, u32[]{:S(2)}, u32[]{:S(2)}) async-start(s32[32,1,32]{2,1,0:T(1,128)} %all_to_all.16), calls=%async_computation | async-start | bytes 32768 | tf_op jit(solution)/shard_map/all_to_all | solution.py:102
  30.0 7.2 %copy-start = (f32[768,1024]{1,0:T(8,128)S(1)}, f32[768,1024]{1,0:T(8,128)}, u32[]{:S(2)}) copy-start(f32[768,1024]{1,0:T(8,128)} %param.13) | copy-start | bytes 9437188
  30.0 32.1 %all-to-all-start.1 = ((bf16[32,32,1024]{2,1,0:T(8,128)(2,1)}), bf16[32,32,1024]{2,1,0:T(8,128)(2,1)}, u32[]{:S(2)}, u32[]{:S(2)}) async-start(bf16[32,32,1024]{2,1,0:T(8,128)(2,1)} %broadcast_select_fusion.1), calls=%async_computation.1 | async-start | bytes 4194304 | tf_op jit(solution)/shard_map/all_to_all | solution.py:104
  36.1 445.8 %all-reduce.6.cloned.1.call-start = ((), (), s32[]{:S(2)}) async-start(), calls=%async_computation.4 | async-start | bytes 7340032 | tf_op jit(solution)/shard_map/psum | solution.py:121
  37.2 1.5 copy-start.5
  44.0 4.0 copy-start.6
  44.0 4.1 copy-start.4
  44.0 4.1 copy-start.3
  100.5 1.6 copy-start.1
  102.1 1.6 copy-start.2
  208.1 277.7 %all-to-all-start.2 = ((bf16[32,32,1024]{2,1,0:T(8,128)(2,1)}), bf16[32,32,1024]{2,1,0:T(8,128)(2,1)}, u32[]{:S(2)}, u32[]{:S(2)}) async-start(bf16[32,32,1024]{2,1,0:T(8,128)(2,1)} %bitcast.13), calls=%async_computation.2 | async-start | bytes 4194304 | tf_op jit(solution)/shard_map/all_to_all | solution.py:111
  215.8 269.5 %copy-start.7 = (f32[768]{0:T(1024)S(1)}, f32[768]{0:T(1024)}, u32[]{:S(2)}) copy-start(f32[768]{0:T(1024)} %param.14) | copy-start | bytes 9220
  215.8 358.3 %all-reduce.4.cloned.1.call-start = ((), (), s32[]{:S(2)}) async-start(), calls=%async_computation.3 | async-start | bytes 2097152 | tf_op jit(solution)/shard_map/psum | solution.py:117
  496.9 2.8 copy-start.9
  502.3 73.3 %copy-start.8 = (f32[512]{0:T(512)S(1)}, f32[512]{0:T(512)}, u32[]{:S(2)}) copy-start(f32[512]{0:T(512)} %param.16) | copy-start | bytes 6148
Sparse Core Ops, SparseCore 0:
  204.4 277.4 all-reduce.5
Sparse Core Ops, SparseCore 1:
  499.8 74.3 all-reduce.3
where the time goes:
time: 596 us; the launch traced here: 589 us
  waiting for transfers between devices  254 us (43%)
  other arithmetic  119 us (20%)
  blocking collectives  94.8 us (16%)
  local copies, waits for them, and re-layouts  70.8 us (12%)
  starting transfers between devices  21.4 us (4%)
  between operations  19 us (3%)
  matrix products  9.25 us (2%)
    psum x1, waiting for transfers between devices, per_device(): lax.psum((hot_grad, relation_grad, loss_sum), ('group', 'member'))  169 us
    psum x1, blocking collectives, per_device(): lax.psum((hot_grad, relation_grad, loss_sum), ('group', 'member'))  94.8 us
    psum x1, waiting for transfers between devices, per_device(): lax.psum(owner_grad.astype(jnp.bfloat16), 'group').astype(jnp.float32)  67.4 us
    scatter-add x1, other arithmetic, device_terms(): entity_grad = entity_grad.at[tail_slots].add(tail_grad)  16.3 us
    all_to_all x1, waiting for transfers between devices, per_device(): lax.all_to_all(served, 'member', split_axis=0, concat_axis=0, tiled=True)  13.9 us
    scatter-add x1, other arithmetic, device_terms(): entity_grad = entity_grad.at[head_slots].add(head_grad)  13.7 us
    gather x2, local copies, waits for them, and re-layouts, device_terms(): head_rows = jnp.take(entity_rows, head_slots, axis=0).astype(jnp.float32)  12.9 us
    gather x2, local copies, waits for them, and re-layouts, device_terms(): tail_rows = jnp.take(entity_rows, tail_slots, axis=0).astype(jnp.float32)  12.5 us
  transfers between devices with their start and end apart: 5, of which 4 were waited for; matrix products, arithmetic and copies ran while one was open for 5% of the time, Pallas kernels for 0%

commit v1 on v0

v1 whole, which is shorter than its diff:
```python
import jax
import jax.numpy as jnp
from jax import lax
from jax.experimental import pallas as pl
from jax.experimental.pallas import tpu as pltpu
from jax.sharding import PartitionSpec as P

learn_rate = 0.1
f32, bf16 = jnp.float32, jnp.bfloat16
TILE = 256
VMEM = pl.BlockSpec(memory_space=pltpu.VMEM)


def dot(lhs, rhs, contract=((1,), (0,))):
    return lax.dot_general(lhs, rhs, (contract, ((), ())), preferred_element_type=f32)


def pick_rows(column, count):
    ids = lax.broadcasted_iota(jnp.int32, (column.shape[0], count), 1)
    return jnp.where(column == ids, 1.0, 0.0).astype(bf16)


def spread_rows(row, first, count):
    ids = lax.broadcasted_iota(jnp.int32, (count, row.shape[1]), 0) + first
    return jnp.where(row == ids, 1.0, 0.0).astype(bf16)


def tiles(total, size=TILE):
    return lambda body: pl.loop(0, total // size)(lambda i: body(pl.ds(pl.multiple_of(i * size, size), size), i))


def serve_kernel(column_ref, table_ref, out_ref, half_ref):
    half_ref[...] = table_ref[...].astype(bf16)

    @tiles(out_ref.shape[0])
    def _(rows, _i):
        hits = pick_rows(column_ref[rows, :], half_ref.shape[0])
        out_ref[rows, :] = dot(hits, half_ref[...]).astype(bf16)


def block_kernel(
    hot_ref, cold_ref, relation_ref, columns_ref, negative_column_ref, slots_ref,
    slot_grad_ref, grads_ref, relation_grads_ref, loss_ref,
    entity, relation_half, heads, tails, relations, negatives, queries, score_grads, pos_grads, query_grads,
):
    hot, half = hot_ref.shape[0], hot_ref.shape[1] // 2
    batch, neg = columns_ref.shape[0], negative_column_ref.shape[0]
    every = entity.shape[0]
    entity[:hot, :] = hot_ref[...].astype(bf16)
    entity[hot:, :] = cold_ref[...]
    relation_half[...] = relation_ref[...].astype(bf16)

    @tiles(neg)
    def _(rows, _i):
        negatives[rows, :] = dot(pick_rows(negative_column_ref[rows, :], every), entity[...]).astype(bf16)

    @tiles(batch)
    def _(rows, _i):
        heads[rows, :] = dot(pick_rows(columns_ref[rows, 0:1], every), entity[...]).astype(bf16)
        tails[rows, :] = dot(pick_rows(columns_ref[rows, 1:2], every), entity[...]).astype(bf16)
        relations[rows, :] = dot(
            pick_rows(columns_ref[rows, 2:3], relation_half.shape[0]), relation_half[...]
        ).astype(bf16)

    def parts(ref, rows):
        both = ref[rows, :].astype(f32)
        return both[:, :half], both[:, half:]

    def query_parts(rows):
        head_real, head_imag = parts(heads, rows)
        relation_real, relation_imag = parts(relations, rows)
        return (
            head_real * relation_real - head_imag * relation_imag,
            head_real * relation_imag + head_imag * relation_real,
        )

    loss_ref[...] = jnp.zeros_like(loss_ref)

    @tiles(batch, 16)
    def _(rows, _i):
        query_real, query_imag = query_parts(rows)
        tail_real, tail_imag = parts(tails, rows)
        positive = jnp.sum(query_real * tail_real + query_imag * tail_imag, -1, keepdims=True)
        queries[rows, :half] = query_real.astype(bf16)
        queries[rows, half:] = query_imag.astype(bf16)
        pos_grads[rows, :] = positive

    positive = pos_grads[...]
    shrunk = jnp.exp(-jnp.abs(positive))
    loss = jnp.sum(jnp.maximum(-positive, 0.0) + jnp.log1p(shrunk))
    pos_grads[...] = jnp.where(positive >= 0, 1.0, shrunk) / (1.0 + shrunk) - 1.0
    loss_ref[...] += loss

    @tiles(batch, 128)
    def _(rows, _i):
        scores = dot(queries[rows, :], negatives[...], ((1,), (1,)))
        shrunk = jnp.exp(-jnp.abs(scores))
        loss = jnp.sum(jnp.maximum(scores, 0.0) + jnp.log1p(shrunk))
        sigmoid = jnp.where(scores >= 0, 1.0, shrunk) / (1.0 + shrunk)
        score_grads[rows, :] = (sigmoid / neg).astype(bf16)
        loss_ref[...] += loss / neg

    @tiles(batch)
    def _(rows, _i):
        query_grads[rows, :] = dot(score_grads[rows, :], negatives[...])

    @tiles(neg)
    def _(rows, i):
        grads_ref[pl.ds(pl.multiple_of(2 * batch + i * TILE, TILE), TILE), :] = dot(
            score_grads[:, pl.ds(pl.multiple_of(i * TILE, TILE), TILE)], queries[...], ((0,), (0,))
        ).astype(bf16)

    @tiles(batch, 16)
    def _(rows, i):
        head_real, head_imag = parts(heads, rows)
        relation_real, relation_imag = parts(relations, rows)
        tail_real, tail_imag = parts(tails, rows)
        pos = pos_grads[rows, :]
        grad_real = query_grads[rows, :half] + pos * tail_real
        grad_imag = query_grads[rows, half:] + pos * tail_imag
        grads_ref[rows, :half] = (grad_real * relation_real + grad_imag * relation_imag).astype(bf16)
        grads_ref[rows, half:] = (grad_imag * relation_real - grad_real * relation_imag).astype(bf16)
        relation_grads_ref[rows, :half] = (grad_real * head_real + grad_imag * head_imag).astype(bf16)
        relation_grads_ref[rows, half:] = (grad_imag * head_real - grad_real * head_imag).astype(bf16)
        later = pl.ds(pl.multiple_of(batch + i * 16, 16), 16)
        grads_ref[later, :half] = (pos * (head_real * relation_real - head_imag * relation_imag)).astype(bf16)
        grads_ref[later, half:] = (pos * (head_real * relation_imag + head_imag * relation_real)).astype(bf16)

    @tiles(every - hot)
    def _(rows, i):
        hits = spread_rows(slots_ref[...], hot + i * TILE, TILE)
        slot_grad_ref[rows, :] = dot(hits, grads_ref[...]).astype(bf16)


def shared_kernel(grads_ref, relation_grads_ref, places_ref, relation_places_ref, loss_ref, out_ref):
    high = loss_ref[...].astype(bf16).astype(f32)
    mid = (loss_ref[...] - high).astype(bf16).astype(f32)
    low = loss_ref[...] - high - mid
    lane = lax.broadcasted_iota(jnp.int32, (1, out_ref.shape[1]), 1)
    pieces = jnp.where(
        lane == 0, high[:1, :1], jnp.where(lane == 1, mid[:1, :1], jnp.where(lane == 2, low[:1, :1], 0.0))
    )

    @tiles(out_ref.shape[0])
    def _(rows, i):
        total = dot(spread_rows(places_ref[...], i * TILE, TILE), grads_ref[...])
        total += dot(spread_rows(relation_places_ref[...], i * TILE, TILE), relation_grads_ref[...])
        place = lax.broadcasted_iota(jnp.int32, (TILE, 1), 0)
        out_ref[rows, :] = jnp.where(place % 32 == 28, pieces, total).astype(bf16)


def owner_kernel(row_ref, arrived_ref, out_ref):
    @tiles(out_ref.shape[0])
    def _(rows, i):
        hits = spread_rows(row_ref[...], i * TILE, TILE)
        out_ref[rows, :] = dot(hits, arrived_ref[...]).astype(bf16)


def params(mib):
    return pltpu.CompilerParams(vmem_limit_bytes=mib * 2**20)


def exchange(array, axis):
    return lax.all_to_all(array, axis, split_axis=0, concat_axis=0, tiled=True)


def adagrad(emb_table, acc_state, row_grad):
    new_state = acc_state + jnp.mean(row_grad * row_grad, -1)
    return (emb_table - learn_rate * row_grad / jnp.sqrt(new_state)[:, None], new_state)


def per_device(
    hot_table, hot_state, cold_table, cold_state, relation_table, relation_state,
    cold_requests, head_slots, relation_index, tail_slots, negative_slots,
):
    members, groups = lax.axis_size("member"), lax.axis_size("group")
    width = hot_table.shape[1]
    hot, owned, relation_count = hot_table.shape[0], cold_table.shape[0], relation_table.shape[0]
    batch, neg = head_slots.shape[0], negative_slots.shape[1]
    asked = cold_requests.shape[1]
    hot_part, relation_part = hot // members, relation_count // members
    shape = jax.ShapeDtypeStruct

    columns = jnp.stack([head_slots, tail_slots, relation_index, relation_index]).T
    slots = jnp.concatenate([head_slots, tail_slots, negative_slots.reshape(-1)])
    places = jnp.where(slots < hot, slots // hot_part * 32 + slots % hot_part, -1).reshape(1, -1)
    slots = slots.reshape(1, -1)
    relation_places = (relation_index // relation_part * 32 + hot_part + relation_index % relation_part).reshape(1, -1)

    received = exchange(cold_requests.reshape(members, -1), "member")
    served = pl.pallas_call(
        serve_kernel, out_shape=shape((asked, width), bf16), in_specs=[VMEM] * 2, out_specs=VMEM,
        scratch_shapes=[pltpu.VMEM((owned, width), bf16)], compiler_params=params(16), name="serve",
    )(received.reshape(-1, 1), cold_table)
    returned = exchange(served.reshape(members, -1, width), "member").reshape(-1, width)

    every = hot + asked
    slot_grads, grads, relation_grads, loss = pl.pallas_call(
        block_kernel,
        out_shape=[
            shape((asked, width), bf16), shape((2 * batch + neg, width), bf16), shape((batch, width), bf16),
            shape((8, 128), f32),
        ],
        in_specs=[VMEM] * 6, out_specs=[VMEM] * 4,
        scratch_shapes=[
            pltpu.VMEM((every, width), bf16), pltpu.VMEM((relation_count, width), bf16),
            pltpu.VMEM((batch, width), bf16), pltpu.VMEM((batch, width), bf16), pltpu.VMEM((batch, width), bf16),
            pltpu.VMEM((neg, width), bf16), pltpu.VMEM((batch, width), bf16), pltpu.VMEM((batch, neg), bf16),
            pltpu.VMEM((batch, 1), f32), pltpu.VMEM((batch, width), f32),
        ],
        compiler_params=params(52), name="block",
    )(hot_table, returned, relation_table, columns, negative_slots.reshape(-1, 1), slots)

    arrived = exchange(slot_grads.reshape(members, -1, width), "member").reshape(-1, width)
    shared = pl.pallas_call(
        shared_kernel, out_shape=shape((32 * members, width), bf16), in_specs=[VMEM] * 5, out_specs=VMEM,
        compiler_params=params(32), name="shared",
    )(grads, relation_grads, places, relation_places, loss)

    owner_grad = pl.pallas_call(
        owner_kernel, out_shape=shape((owned, width), bf16), in_specs=[VMEM] * 2, out_specs=VMEM,
        compiler_params=params(16), name="owner",
    )(received.reshape(1, -1), arrived)
    cold_pieces = exchange(owner_grad.reshape(groups, -1, width), "group")
    cold_piece = jnp.sum(cold_pieces.astype(f32), 0).astype(bf16)
    cold_total = exchange(jnp.broadcast_to(cold_piece[None], (groups,) + cold_piece.shape), "group")
    cold_total = cold_total.reshape(owned, width).astype(f32)

    shared = exchange(shared.reshape(members, -1, width), "member")
    shared = jnp.sum(shared.astype(f32), 0)
    loss = jnp.sum(shared[28])
    high = lax.reduce_precision(loss, 8, 7)
    mid = lax.reduce_precision(loss - high, 8, 7)
    lane = jnp.arange(width)
    pieces = jnp.where(lane == 0, high, jnp.where(lane == 1, mid, jnp.where(lane == 2, loss - high - mid, 0.0)))
    shared = jnp.where(jnp.arange(32)[:, None] == 28, pieces[None], shared).astype(bf16)
    shared = exchange(jnp.broadcast_to(shared[None], (groups,) + shared.shape), "group")
    shared = jnp.sum(shared.astype(f32), 0)
    mean_loss = jnp.sum(shared[28]) / (batch * groups * members)
    shared = shared.astype(bf16)
    shared = exchange(jnp.broadcast_to(shared[None], (members,) + shared.shape), "member").astype(f32)
    hot_total = shared[:, :hot_part].reshape(hot, width)
    relation_total = shared[:, hot_part : hot_part + relation_part].reshape(relation_count, width)

    new_cold_table, new_cold_state = adagrad(cold_table, cold_state, cold_total)
    new_hot_table, new_hot_state = adagrad(hot_table, hot_state, hot_total)
    new_relation_table, new_relation_state = adagrad(relation_table, relation_state, relation_total)
    return (
        new_hot_table, new_hot_state, new_cold_table, new_cold_state,
        new_relation_table, new_relation_state, mean_loss,
    )


def solution(mesh):
    placed = (
        P(), P(), P("member", None), P("member"), P(), P(), P(("group", "member"), None),
        P(("group", "member")), P(("group", "member")), P(("group", "member")), P(("group", "member"), None),
    )
    return jax.shard_map(
        per_device, mesh=mesh, in_specs=placed,
        out_specs=(P(), P(), P("member", None), P("member"), P(), P(), P()), check_vma=False,
    )
```

time: 596 us -> 315 us (0.53); the launches traced: 589 us -> 314 us
  waiting for transfers between devices: 254 us -> 127 us
  other arithmetic: 119 us -> 27 us
  Pallas kernels: 0 us -> 58.8 us
  local copies, waits for them, and re-layouts: 70.8 us -> 14.6 us
  blocking collectives: 94.8 us -> 46 us
  starting transfers between devices: 21.4 us -> 34.2 us
  between operations: 19 us -> 6.31 us
  matrix products: 9.25 us -> 0 us
    psum x2 -> x0, waiting for transfers between devices: 236 us -> none  [the longest x1 169 us: per_device(): lax.psum((hot_grad, relation_grad, loss_sum), ('group', 'member'))]
    all_to_all x3 -> x6, waiting for transfers between devices: 18.3 us -> 127 us  [exchange(): return lax.all_to_all(array, axis, split_axis=0, concat_axis=0, tiled=True)]
    psum x1 -> x0, blocking collectives: 94.8 us -> none  [per_device(): lax.psum((hot_grad, relation_grad, loss_sum), ('group', 'member'))]
    scatter-add x5 -> x0, other arithmetic: 64.1 us -> none  [the longest x1 16.3 us: device_terms(): entity_grad = entity_grad.at[tail_slots].add(tail_grad)]
    pallas_call x0 -> x4, Pallas kernels: none -> 58.8 us  [the longest x1 44.6 us: per_device(): pl.pallas_call(block_kernel, out_shape=[shape((asked, width), bf16), shap...]
    all_to_all x0 -> x2, blocking collectives: none -> 46 us  [exchange(): return lax.all_to_all(array, axis, split_axis=0, concat_axis=0, tiled=True)]
    gather x8 -> x0, local copies, waits for them, and re-layouts: 44.7 us -> none  [the longest x2 12.9 us: device_terms(): head_rows = jnp.take(entity_rows, head_slots, axis=0).astype(jnp.float32)]
    concatenate x3 -> x1, other arithmetic: 13.2 us -> 0.01 us  [per_device(): jnp.concatenate([head_slots, tail_slots, negative_slots.reshape(-1)])]
  transfers between devices with their start and end apart: 5 -> 6, of which waited for: 4 -> 6; matrix products, arithmetic and copies ran while one was open for 5% -> 6% of each run, Pallas kernels for 0% -> 1%
where the time goes in v1:
time: 315 us; the launch traced here: 314 us
  waiting for transfers between devices  127 us (40%)
  Pallas kernels  58.8 us (19%)
  blocking collectives  46 us (15%)
  starting transfers between devices  34.2 us (11%)
  other arithmetic  27 us (9%)
  local copies, waits for them, and re-layouts  14.6 us (5%)
  between operations  6.31 us (2%)
    all_to_all x6, waiting for transfers between devices, exchange(): return lax.all_to_all(array, axis, split_axis=0, concat_axis=0, tiled=True)  127 us
    all_to_all x2, blocking collectives, exchange(): return lax.all_to_all(array, axis, split_axis=0, concat_axis=0, tiled=True)  46 us
    pallas_call x1, Pallas kernels, per_device(): pl.pallas_call(block_kernel, out_shape=[shape((asked, width), bf16), shap...  44.6 us
    all_to_all x6, starting transfers between devices, exchange(): return lax.all_to_all(array, axis, split_axis=0, concat_axis=0, tiled=True)  34.2 us
    sub x3, other arithmetic, adagrad(): emb_table - learn_rate * row_grad / jnp.sqrt(new_state)[:, None]  9.64 us
    unnamed x31, local copies, waits for them, and re-layouts  9.48 us
    pallas_call x1, Pallas kernels, per_device(): pl.pallas_call(shared_kernel, out_shape=shape((32 * members, width), bf16...  8.44 us
    reduce_sum x3, other arithmetic, adagrad(): new_state = acc_state + jnp.mean(row_grad * row_grad, -1)  6.92 us
  transfers between devices with their start and end apart: 6, of which 6 were waited for; matrix products, arithmetic and copies ran while one was open for 6% of the time, Pallas kernels for 1%

profile of v1, /device:TPU:2, one launch (start us, length us, event | category | flops | bytes accessed | tf_op | source)
XLA Modules:
  0.0 313.7 jit_solution(11977413530483063730)
XLA Ops:
  0.6 0.5 broadcast.171
  1.1 1.3 reduce.14
  2.6 13.6 %all_to_all.44 = s32[32,1,32]{2,1,0:T(1,128)S(1)} all-to-all(s32[32,1,32]{2,1,0:T(1,128)S(1)} %all_to_all.27), channel_id=1, replica_groups=mesh['group'=8,'member'=32] {'member'}, dimensions={0} | all-to-all | bytes 8192 | tf_op jit(solution)/shard_map/all_to_all | solution.py:164
  16.2 0.7 reduce.15
  16.9 0.5 reshape.325.column_ref
  17.4 1.6 copy-done
  19.0 3.4 %serve.1 = bf16[1024,1024]{1,0:T(8,128)(2,1)} custom-call(s32[1024,1]{1,0:T(8,128)S(1)} %reshape.325.column_ref, f32[512,1024]{1,0:T(8,128)S(1)} %copy-done), custom_call_target="tpu_custom_call" | custom-call | tf_op jit(solution)/shard_map/serve/pallas_call | solution.py:191
  22.4 5.3 %all-to-all-start.1 = ((bf16[32,32,1024]{2,1,0:T(8,128)(2,1)}), bf16[32,32,1024]{2,1,0:T(8,128)(2,1)S(1)}, u32[]{:S(2)}, u32[]{:S(2)}) async-start(bf16[32,32,1024]{2,1,0:T(8,128)(2,1)} %bitcast), calls=%async_computation.1 | async-start | bytes 4194304 | tf_op jit(solution)/shard_map/all_to_all | solution.py:164
  27.8 0.2 copy.26.columns_ref
  28.0 0.1 copy.27.negative_column_ref
  28.3 25.3 %all-to-all-done.1 = bf16[32,32,1024]{2,1,0:T(8,128)(2,1)S(1)} async-done(((bf16[32,32,1024]{2,1,0:T(8,128)(2,1)}), bf16[32,32,1024]{2,1,0:T(8,128)(2,1)S(1)}, u32[]{:S(2)}, u32[]{:S(2)}) %all-to-all-start.1) | async-done | bytes 2097184 | tf_op jit(solution)/shard_map/all_to_all | solution.py:164
  53.6 1.3 copy-done.6
  55.0 44.6 %block.1 = (bf16[1024,1024]{1,0:T(8,128)(2,1)}, bf16[2560,1024]{1,0:T(8,128)(2,1)}, bf16[1024,1024]{1,0:T(8,128)(2,1)}, f32[8,128]{1,0:T(8,128)S(1)}) custom-call(f32[768,1024]{1,0:T(8,128)} %hot_ref.1, bf16[1024,1024]{1,0:T(8,128)(2,1)} %bitcast.26, f32[128,1024]{1,0:T(8,128)S(1)} %copy-done.3, s32[1024,4]{1,0:T(8,128)S(1)} %copy.26.columns_ref, ...), custom_call_target="tpu_custom_call" | custom-call | tf_op jit(solution)/shard_map/block/pallas_call | solution.py:198
  99.5 2.5 copy-done.2
  102.0 1.6 copy-done.4
  103.6 8.4 %shared.1 = bf16[1024,1024]{1,0:T(8,128)(2,1)S(1)} custom-call(bf16[2560,1024]{1,0:T(8,128)(2,1)S(1)} %copy-done.2, bf16[1024,1024]{1,0:T(8,128)(2,1)S(1)} %copy-done.4, s32[1,2560]{1,0:T(1,128)S(1)} %compare_select_fusion.places_ref, s32[1,1024]{1,0:T(1,128)S(1)} %bitcast.25, f32[8,128]{1,0:T(8,128)S(1)} %get-tuple-element.13.loss_ref), custom_call_target="tpu_custom_call" | custom-call | tf_op jit(solution)/shard_map/shared/pallas_call | solution.py:215
  112.1 32.4 %all_to_all.45 = bf16[32,32,1024]{2,1,0:T(8,128)(2,1)} all-to-all(bf16[32,32,1024]{2,1,0:T(8,128)(2,1)S(1)} %bitcast.24), channel_id=1, replica_groups=mesh['group'=8,'member'=32] {'member'}, dimensions={0} | all-to-all | bytes 4194304 | tf_op jit(solution)/shard_map/all_to_all | solution.py:164
  144.4 6.4 %all-to-all-start.5 = ((bf16[32,32,1024]{2,1,0:T(8,128)(2,1)}), bf16[32,32,1024]{2,1,0:T(8,128)(2,1)S(1)}, u32[]{:S(2)}, u32[]{:S(2)}) async-start(bf16[32,32,1024]{2,1,0:T(8,128)(2,1)} %bitcast.27), calls=%async_computation.5 | async-start | bytes 4194304 | tf_op jit(solution)/shard_map/all_to_all | solution.py:164
  150.8 2.0 convert_reduce_fusion
  152.8 0.6 slice_reduce_fusion.1
  157.0 1.3 select_select_fusion
  158.4 18.4 %all-to-all-done.5 = bf16[32,32,1024]{2,1,0:T(8,128)(2,1)S(1)} async-done(((bf16[32,32,1024]{2,1,0:T(8,128)(2,1)}), bf16[32,32,1024]{2,1,0:T(8,128)(2,1)S(1)}, u32[]{:S(2)}, u32[]{:S(2)}) %all-to-all-start.5) | async-done | bytes 2097184 | tf_op jit(solution)/shard_map/all_to_all | solution.py:164
  176.8 0.9 broadcast_in_dim.62
  177.6 8.5 %all-to-all-start.3 = ((bf16[8,32,1024]{2,1,0:T(8,128)(2,1)}), bf16[8,32,1024]{2,1,0:T(8,128)(2,1)S(1)}, u32[]{:S(2)}, u32[]{:S(2)}) async-start(bf16[8,32,1024]{2,1,0:T(8,128)(2,1)} %broadcast_in_dim.62), calls=%async_computation.3 | async-start | bytes 1048576 | tf_op jit(solution)/shard_map/all_to_all | solution.py:164
  186.2 2.4 owner.1
  188.6 15.5 %all-to-all-done.3 = bf16[8,32,1024]{2,1,0:T(8,128)(2,1)S(1)} async-done(((bf16[8,32,1024]{2,1,0:T(8,128)(2,1)}), bf16[8,32,1024]{2,1,0:T(8,128)(2,1)S(1)}, u32[]{:S(2)}, u32[]{:S(2)}) %all-to-all-start.3) | async-done | bytes 524320 | tf_op jit(solution)/shard_map/all_to_all | solution.py:164
  204.1 3.6 %all-to-all-start.6 = ((bf16[8,64,1024]{2,1,0:T(8,128)(2,1)}), bf16[8,64,1024]{2,1,0:T(8,128)(2,1)S(1)}, u32[]{:S(2)}, u32[]{:S(2)}) async-start(bf16[8,64,1024]{2,1,0:T(8,128)(2,1)} %bitcast.13), calls=%async_computation.6 | async-start | bytes 2097152 | tf_op jit(solution)/shard_map/all_to_all | solution.py:164
  207.8 29.1 %all-to-all-done.6 = bf16[8,64,1024]{2,1,0:T(8,128)(2,1)S(1)} async-done(((bf16[8,64,1024]{2,1,0:T(8,128)(2,1)}), bf16[8,64,1024]{2,1,0:T(8,128)(2,1)S(1)}, u32[]{:S(2)}, u32[]{:S(2)}) %all-to-all-start.6) | async-done | bytes 1048608 | tf_op jit(solution)/shard_map/all_to_all | solution.py:164
  236.8 1.7 broadcast_in_dim.63
  238.5 6.3 %all-to-all-start.4 = ((bf16[32,32,1024]{2,1,0:T(8,128)(2,1)}), bf16[32,32,1024]{2,1,0:T(8,128)(2,1)S(1)}, u32[]{:S(2)}, u32[]{:S(2)}) async-start(bf16[32,32,1024]{2,1,0:T(8,128)(2,1)} %broadcast_in_dim.63), calls=%async_computation.4 | async-start | bytes 4194304 | tf_op jit(solution)/shard_map/all_to_all | solution.py:164
  244.8 0.6 slice_reduce_fusion
  246.0 1.4 reduce_sum.79
  247.5 23.3 %all-to-all-done.4 = bf16[32,32,1024]{2,1,0:T(8,128)(2,1)S(1)} async-done(((bf16[32,32,1024]{2,1,0:T(8,128)(2,1)}), bf16[32,32,1024]{2,1,0:T(8,128)(2,1)S(1)}, u32[]{:S(2)}, u32[]{:S(2)}) %all-to-all-start.4) | async-done | bytes 2097184 | tf_op jit(solution)/shard_map/all_to_all | solution.py:164
  270.7 1.1 broadcast_in_dim.64
  271.8 4.2 %all-to-all-start.7 = ((bf16[8,64,1024]{2,1,0:T(8,128)(2,1)}), bf16[8,64,1024]{2,1,0:T(8,128)(2,1)}, u32[]{:S(2)}, u32[]{:S(2)}) async-start(bf16[8,64,1024]{2,1,0:T(8,128)(2,1)} %broadcast_in_dim.64), calls=%async_computation.7 | async-start | bytes 2097152 | tf_op jit(solution)/shard_map/all_to_all | solution.py:164
  276.1 0.5 convert_element_type.34
  276.6 1.9 copy-done.5
  278.5 0.2 multiply_reduce_fusion.1
  278.7 0.2 mul.72
  279.0 3.9 %multiply_reduce_fusion = (f32[32,24]{1,0:T(8,128)S(1)}, f32[32,24,1024]{2,1,0:T(8,128)}) fusion(f32[32,32,1024]{2,1,0:T(8,128)} %copy-done.5), kind=kLoop, calls=%fused_computation.3 | loop fusion | flops 2358528 | bytes 6294528 | tf_op jit(solution)/shard_map/reduce_sum | solution.py:168
  283.0 0.5 fusion.11
  283.6 0.6 fusion.13
  284.1 0.9 divide_subtract_fusion
  285.1 5.4 %fusion = f32[768,1024]{1,0:T(8,128)} fusion(f32[768,1024]{1,0:T(8,128)} %hot_ref.1, f32[32,24,1024]{2,1,0:T(8,128)} %get-tuple-element.24, f32[768]{0:T(1024)S(1)} %get-tuple-element.19), kind=kLoop, calls=%fused_computation.2 | loop fusion | flops 1572864 | bytes 9440256 | tf_op jit(solution)/shard_map/sub | solution.py:169
  290.5 15.3 %all-to-all-done.7 = bf16[8,64,1024]{2,1,0:T(8,128)(2,1)} async-done(((bf16[8,64,1024]{2,1,0:T(8,128)(2,1)}), bf16[8,64,1024]{2,1,0:T(8,128)(2,1)}, u32[]{:S(2)}, u32[]{:S(2)}) %all-to-all-start.7) | async-done | bytes 1048608 | tf_op jit(solution)/shard_map/all_to_all | solution.py:164
  305.7 2.8 fusion.1
  308.6 0.6 fusion.12
  309.2 3.3 %fusion.2 = f32[512,1024]{1,0:T(8,128)} fusion(f32[512,1024]{1,0:T(8,128)S(1)} %copy-done.1, f32[8,64,1024]{2,1,0:T(8,128)} %get-tuple-element.26, f32[512]{0:T(512)S(1)} %get-tuple-element.17), kind=kLoop, calls=%fused_computation.9 | loop fusion | flops 1048576 | bytes 6293504 | tf_op jit(solution)/shard_map/sub | solution.py:169
  (42 shorter events, 0.8 us)
Async XLA Ops:
  17.4 1.6 copy-start
  22.4 5.3 %copy-start.8 = (s32[1024]{0:T(1024)S(1)}, s32[1024]{0:T(1024)}, u32[]{:S(2)}) copy-start(s32[1024]{0:T(1024)} %param.20) | copy-start | bytes 12292
  22.4 5.3 %copy-start.9 = (s32[1024]{0:T(1024)S(1)}, s32[1024]{0:T(1024)}, u32[]{:S(2)}) copy-start(s32[1024]{0:T(1024)} %param.18) | copy-start | bytes 12292
  22.4 5.3 %copy-start.11 = (s32[1024]{0:T(1024)S(1)}, s32[1024]{0:T(1024)}, u32[]{:S(2)}) copy-start(s32[1024]{0:T(1024)} %param.19) | copy-start | bytes 12292
  22.4 5.6 %copy-start.10 = (s32[1,512]{1,0:T(1,128)S(1)}, s32[1,512]{1,0:T(1,128)}, u32[]{:S(2)}) copy-start(s32[1,512]{1,0:T(1,128)} %param.21) | copy-start | bytes 6148
  22.4 32.6 %copy-start.3 = (f32[128,1024]{1,0:T(8,128)S(1)}, f32[128,1024]{1,0:T(8,128)}, u32[]{:S(2)}) copy-start(f32[128,1024]{1,0:T(8,128)} %relation_ref.1) | copy-start | bytes 1572868
  22.4 31.2 %all-to-all-start.1 = ((bf16[32,32,1024]{2,1,0:T(8,128)(2,1)}), bf16[32,32,1024]{2,1,0:T(8,128)(2,1)S(1)}, u32[]{:S(2)}, u32[]{:S(2)}) async-start(bf16[32,32,1024]{2,1,0:T(8,128)(2,1)} %bitcast), calls=%async_computation.1 | async-start | bytes 4194304 | tf_op jit(solution)/shard_map/all_to_all | solution.py:164
  53.6 1.3 copy-start.6
  99.5 2.5 copy-start.2
  102.0 1.6 copy-start.4
  144.4 32.3 %all-to-all-start.5 = ((bf16[32,32,1024]{2,1,0:T(8,128)(2,1)}), bf16[32,32,1024]{2,1,0:T(8,128)(2,1)S(1)}, u32[]{:S(2)}, u32[]{:S(2)}) async-start(bf16[32,32,1024]{2,1,0:T(8,128)(2,1)} %bitcast.27), calls=%async_computation.5 | async-start | bytes 4194304 | tf_op jit(solution)/shard_map/all_to_all | solution.py:164
  177.6 26.5 %all-to-all-start.3 = ((bf16[8,32,1024]{2,1,0:T(8,128)(2,1)}), bf16[8,32,1024]{2,1,0:T(8,128)(2,1)S(1)}, u32[]{:S(2)}, u32[]{:S(2)}) async-start(bf16[8,32,1024]{2,1,0:T(8,128)(2,1)} %broadcast_in_dim.62), calls=%async_computation.3 | async-start | bytes 1048576 | tf_op jit(solution)/shard_map/all_to_all | solution.py:164
  204.1 32.7 %all-to-all-start.6 = ((bf16[8,64,1024]{2,1,0:T(8,128)(2,1)}), bf16[8,64,1024]{2,1,0:T(8,128)(2,1)S(1)}, u32[]{:S(2)}, u32[]{:S(2)}) async-start(bf16[8,64,1024]{2,1,0:T(8,128)(2,1)} %bitcast.13), calls=%async_computation.6 | async-start | bytes 2097152 | tf_op jit(solution)/shard_map/all_to_all | solution.py:164
  236.8 1.7 copy-start.7
  238.5 32.3 %all-to-all-start.4 = ((bf16[32,32,1024]{2,1,0:T(8,128)(2,1)}), bf16[32,32,1024]{2,1,0:T(8,128)(2,1)S(1)}, u32[]{:S(2)}, u32[]{:S(2)}) async-start(bf16[32,32,1024]{2,1,0:T(8,128)(2,1)} %broadcast_in_dim.63), calls=%async_computation.4 | async-start | bytes 4194304 | tf_op jit(solution)/shard_map/all_to_all | solution.py:164
  271.8 33.9 %all-to-all-start.7 = ((bf16[8,64,1024]{2,1,0:T(8,128)(2,1)}), bf16[8,64,1024]{2,1,0:T(8,128)(2,1)}, u32[]{:S(2)}, u32[]{:S(2)}) async-start(bf16[8,64,1024]{2,1,0:T(8,128)(2,1)} %broadcast_in_dim.64), calls=%async_computation.7 | async-start | bytes 2097152 | tf_op jit(solution)/shard_map/all_to_all | solution.py:164
  276.6 1.9 copy-start.5
  279.0 4.0 %copy-start.14 = (f32[128]{0:T(128)S(1)}, f32[128]{0:T(128)}, u32[]{:S(2)}) copy-start(f32[128]{0:T(128)} %param.16) | copy-start | bytes 1540
  279.0 4.5 %copy-start.12 = (f32[768]{0:T(1024)S(1)}, f32[768]{0:T(1024)}, u32[]{:S(2)}) copy-start(f32[768]{0:T(1024)} %param.12) | copy-start | bytes 9220
  290.5 18.2 %copy-start.13 = (f32[512]{0:T(512)S(1)}, f32[512]{0:T(512)}, u32[]{:S(2)}) copy-start(f32[512]{0:T(512)} %param.14) | copy-start | bytes 6148
  290.5 18.8 %copy-start.1 = (f32[512,1024]{1,0:T(8,128)S(1)}, f32[512,1024]{1,0:T(8,128)}, u32[]{:S(2)}) copy-start(f32[512,1024]{1,0:T(8,128)} %table_ref.1) | copy-start | bytes 6291460

commit v2 on v1

v2 whole, which is shorter than its diff:
```python
import functools

import jax
import jax.numpy as jnp
from jax import lax
from jax.experimental import pallas as pl
from jax.experimental.pallas import tpu as pltpu
from jax.sharding import PartitionSpec as P

learn_rate = 0.1
f32, bf16 = jnp.float32, jnp.bfloat16
TILE = 512
STRIP = 16
BUNDLE = 32
LANES = 128
VMEM = pl.BlockSpec(memory_space=pltpu.VMEM)
HBM = pl.BlockSpec(memory_space=pltpu.HBM)
shape = jax.ShapeDtypeStruct


def dot(lhs, rhs, contract=((1,), (0,))):
    return lax.dot_general(lhs, rhs, (contract, ((), ())), preferred_element_type=f32)


def pick_rows(column, first, count):
    ids = lax.broadcasted_iota(jnp.int32, (column.shape[0], count), 1) + first
    return jnp.where(column == ids, 1.0, 0.0).astype(bf16)


def spread_rows(row, ids):
    return jnp.where(row == ids, 1.0, 0.0).astype(bf16)


def row_ids(first, count, width):
    return lax.broadcasted_iota(jnp.int32, (count, width), 0) + first


def at(i, size):
    return pl.ds(pl.multiple_of(i * size, size), size)


def diagonal(count):
    ids = [lax.broadcasted_iota(jnp.int32, (count, count), k) for k in (0, 1)]
    return ids[0] == ids[1]


def to_column(row):
    return jnp.sum(jnp.where(diagonal(row.shape[1]), row, 0.0), 1, keepdims=True)


def to_row(column):
    return jnp.sum(jnp.where(diagonal(column.shape[0]), column, 0.0), 0, keepdims=True)


def serve_kernel(received_ref, half_ref, out_ref, hits, rows_out, sems):
    members, slots = received_ref.shape
    owned = half_ref.shape[0]
    ids = lax.broadcasted_iota(jnp.int32, (slots, owned), 1).astype(f32)
    received = received_ref[...].astype(f32)
    copies = []
    for first in range(0, members * slots, TILE):
        for member in range(first // slots, (first + TILE) // slots):
            column = to_column(received[member : member + 1, :])
            hits[member * slots : (member + 1) * slots, :] = jnp.where(column == ids, 1.0, 0.0).astype(bf16)
        rows = pl.ds(first, TILE)
        rows_out[rows, :] = dot(hits[rows, :], half_ref[...]).astype(bf16)
        copies.append(pltpu.make_async_copy(rows_out.at[rows], out_ref.at[rows], sems.at[first // TILE]))
        copies[-1].start()
    for copy in copies:
        copy.wait()


def early_kernel(hot_ref, relation_ref, columns_ref, negative_column_ref, heads_ref, tails_ref, negatives_ref, relations_ref):
    hot, kinds = hot_ref.shape[0], relation_ref.shape[0]

    @pl.loop(0, negatives_ref.shape[0] // TILE)
    def _(i):
        rows = at(i, TILE)
        negatives_ref[rows, :] = dot(pick_rows(negative_column_ref[rows, :], 0, hot), hot_ref[...]).astype(bf16)

    @pl.loop(0, heads_ref.shape[0] // TILE)
    def _(i):
        rows = at(i, TILE)
        heads_ref[rows, :] = dot(pick_rows(columns_ref[rows, 0:1], 0, hot), hot_ref[...]).astype(bf16)
        tails_ref[rows, :] = dot(pick_rows(columns_ref[rows, 1:2], 0, hot), hot_ref[...]).astype(bf16)
        relations_ref[rows, :] = dot(pick_rows(columns_ref[rows, 2:3], 0, kinds), relation_ref[...]).astype(bf16)


def block_kernel(
    cold_hbm, heads_hbm, tails_hbm, negatives_hbm, relations_hbm, columns_hbm, negative_column_hbm, slots_ref,
    slot_grad_hbm, grads_hbm, relation_grads_hbm, loss_ref,
    cold_ref, heads, tails, negatives, relations, columns_ref, negative_column_ref,
    grads_ref, relation_grads_ref, slot_grad_ref, queries, score_grads, pos_grads, query_grads, sems_in, sems_out,
):
    batch, width = heads.shape
    neg, asked, half = negatives.shape[0], cold_ref.shape[0], width // 2
    hot = 768
    pairs = (
        (cold_hbm, cold_ref), (negative_column_hbm, negative_column_ref), (negatives_hbm, negatives),
        (columns_hbm, columns_ref), (heads_hbm, heads), (tails_hbm, tails), (relations_hbm, relations),
    )
    copies = [pltpu.make_async_copy(source, target, sems_in.at[k]) for k, (source, target) in enumerate(pairs)]
    for copy in copies:
        copy.start()
    for copy in copies[:3]:
        copy.wait()

    def add_cold(target, column_ref, lane):
        @pl.loop(0, target.shape[0] // TILE)
        def _(i):
            rows = at(i, TILE)
            found = dot(pick_rows(column_ref[rows, lane : lane + 1], hot, asked), cold_ref[...])
            target[rows, :] = (found + target[rows, :].astype(f32)).astype(bf16)

    add_cold(negatives, negative_column_ref, 0)
    for copy in copies[3:]:
        copy.wait()
    add_cold(heads, columns_ref, 0)
    add_cold(tails, columns_ref, 1)

    def parts(ref, rows):
        both = ref[rows, :].astype(f32)
        return both[:, :half], both[:, half:]

    @pl.loop(0, batch // STRIP, unroll=4)
    def _(i):
        rows = at(i, STRIP)
        head_real, head_imag = parts(heads, rows)
        relation_real, relation_imag = parts(relations, rows)
        query_real = head_real * relation_real - head_imag * relation_imag
        query_imag = head_real * relation_imag + head_imag * relation_real
        tail_real, tail_imag = parts(tails, rows)
        queries[rows, :half] = query_real.astype(bf16)
        queries[rows, half:] = query_imag.astype(bf16)
        pos_grads[rows, :] = jnp.sum(query_real * tail_real + query_imag * tail_imag, -1, keepdims=True)

    positive = pos_grads[...]
    shrunk = jnp.exp(-jnp.abs(positive))
    loss_ref[...] = jnp.full_like(loss_ref, jnp.sum(jnp.maximum(-positive, 0.0) + jnp.log1p(shrunk)))
    pos_grads[...] = jnp.where(positive >= 0, 1.0, shrunk) / (1.0 + shrunk) - 1.0

    @pl.loop(0, batch // 128, unroll=2)
    def _(i):
        rows = at(i, 128)
        scores = dot(queries[rows, :], negatives[...], ((1,), (1,)))
        shrunk = jnp.exp(-jnp.abs(scores))
        loss = jnp.sum(jnp.maximum(scores, 0.0) + jnp.log1p(shrunk))
        sigmoid = jnp.where(scores >= 0, 1.0, shrunk) / (1.0 + shrunk)
        score_grads[rows, :] = (sigmoid / neg).astype(bf16)
        loss_ref[...] += loss / neg

    @pl.loop(0, batch // TILE)
    def _(i):
        rows = at(i, TILE)
        query_grads[rows, :] = dot(score_grads[rows, :], negatives[...])

    grads_ref[2 * batch :, :] = dot(score_grads[...], queries[...], ((0,), (0,))).astype(bf16)

    @pl.loop(0, batch // STRIP, unroll=4)
    def _(i):
        rows = at(i, STRIP)
        head_real, head_imag = parts(heads, rows)
        relation_real, relation_imag = parts(relations, rows)
        tail_real, tail_imag = parts(tails, rows)
        pos = pos_grads[rows, :]
        grad_real = query_grads[rows, :half] + pos * tail_real
        grad_imag = query_grads[rows, half:] + pos * tail_imag
        grads_ref[rows, :half] = (grad_real * relation_real + grad_imag * relation_imag).astype(bf16)
        grads_ref[rows, half:] = (grad_imag * relation_real - grad_real * relation_imag).astype(bf16)
        relation_grads_ref[rows, :half] = (grad_real * head_real + grad_imag * head_imag).astype(bf16)
        relation_grads_ref[rows, half:] = (grad_imag * head_real - grad_real * head_imag).astype(bf16)
        later = pl.ds(pl.multiple_of(batch + i * STRIP, STRIP), STRIP)
        grads_ref[later, :half] = (pos * (head_real * relation_real - head_imag * relation_imag)).astype(bf16)
        grads_ref[later, half:] = (pos * (head_real * relation_imag + head_imag * relation_real)).astype(bf16)

    copies = [
        pltpu.make_async_copy(grads_ref, grads_hbm, sems_out.at[0]),
        pltpu.make_async_copy(relation_grads_ref, relation_grads_hbm, sems_out.at[1]),
    ]
    for copy in copies:
        copy.start()
    for i in range(asked // TILE):
        rows = pl.ds(i * TILE, TILE)
        hits = spread_rows(slots_ref[...], row_ids(hot + i * TILE, TILE, 1))
        slot_grad_ref[rows, :] = dot(hits, grads_ref[...]).astype(bf16)
        copies.append(pltpu.make_async_copy(slot_grad_ref.at[rows], slot_grad_hbm.at[rows], sems_out.at[2 + i]))
        copies[-1].start()
    for copy in copies:
        copy.wait()


def loss_pieces(loss, width):
    high = loss.astype(bf16).astype(f32)
    mid = (loss - high).astype(bf16).astype(f32)
    lane = lax.broadcasted_iota(jnp.int32, (1, width), 1)
    return jnp.where(lane == 0, high, jnp.where(lane == 1, mid, jnp.where(lane == 2, loss - high - mid, 0.0)))


def shared_kernel(loss_at, grads_ref, relation_grads_ref, places_ref, relation_places_ref, loss_ref, mine_ref, other_ref):
    count, width = mine_ref.shape
    pieces = loss_pieces(loss_ref[:1, :1], width)
    place = row_ids(0, count, 1)
    for i, out_ref in enumerate((mine_ref, other_ref)):
        ids = row_ids(i * count, count, 1)
        total = dot(spread_rows(places_ref[...], ids), grads_ref[...])
        total += dot(spread_rows(relation_places_ref[...], ids), relation_grads_ref[...])
        out_ref[...] = jnp.where(place % BUNDLE == loss_at, pieces, total).astype(out_ref.dtype)


def total_of(parts):
    return sum((part.astype(f32) for part in parts[1:]), parts[0].astype(f32))


def owner_kernel(row_ref, arrived_ref, mine_ref, other_ref, owner_ref, shared_ref):
    shared_ref[...] = (mine_ref[...] + other_ref[...].astype(f32)).astype(bf16)
    hits = spread_rows(row_ref[...], row_ids(0, owner_ref.shape[0], 1))
    owner_ref[...] = dot(hits, arrived_ref[...]).astype(bf16)


def member_sum_kernel(loss_at, parts_ref, out_ref):
    total = total_of([parts_ref[k] for k in range(parts_ref.shape[0])])
    loss = jnp.sum(total[loss_at : loss_at + 1, :], -1, keepdims=True)
    total = jnp.where(row_ids(0, BUNDLE, 1) == loss_at, loss_pieces(loss, total.shape[1]), total).astype(bf16)
    for k in range(out_ref.shape[0]):
        out_ref[k] = total


def group_sum_kernel(loss_at, batch_total, parts_ref, _after, shared_ref, loss_ref):
    total = total_of([parts_ref[k] for k in range(parts_ref.shape[0])])
    loss = jnp.sum(total[loss_at : loss_at + 1, :], -1, keepdims=True)
    loss_ref[...] = jnp.broadcast_to(loss / batch_total, loss_ref.shape)
    total = total.astype(bf16)
    for k in range(shared_ref.shape[0]):
        shared_ref[k] = total


def stepped(table, state_row, grad):
    new_state = to_column(state_row) + jnp.mean(grad * grad, -1, keepdims=True)
    return table - learn_rate * grad / jnp.sqrt(new_state), to_row(new_state)


def cold_step_kernel(grad_ref, table_ref, state_ref, new_table, new_state):
    at_row = pl.ds(pl.program_id(0), 1)
    new_table[...], new_state[at_row, :] = stepped(table_ref[...], state_ref[at_row, :], grad_ref[...].astype(f32))


def shared_step_kernel(
    shared_ref, hot_ref, hot_state_ref, relation_ref, relation_state_ref,
    new_hot, new_hot_state, new_relation, new_relation_state, grads,
):
    step = pl.program_id(0)

    @pl.when(step == 0)
    def _():
        members = shared_ref.shape[0] // BUNDLE
        hot_part, relation_part = grads.shape[0] // members, relation_ref.shape[0] // members
        relation_grad = []
        for member in range(members):
            bundle = shared_ref[member * BUNDLE : (member + 1) * BUNDLE, :].astype(f32)
            grads[member * hot_part : (member + 1) * hot_part, :] = bundle[:hot_part, :]
            relation_grad.append(bundle[hot_part : hot_part + relation_part, :])
        new_relation[...], new_relation_state[...] = stepped(
            relation_ref[...], relation_state_ref[...], jnp.concatenate(relation_grad)
        )

    at_row = pl.ds(step, 1)
    new_hot[...], new_hot_state[at_row, :] = stepped(hot_ref[...], hot_state_ref[at_row, :], grads[at(step, LANES), :])


def call(kernel, name, out_shape, args, mib, flops=0, in_spaces=None, out_spaces=None, scratch=()):
    several = isinstance(out_shape, list)
    out_spaces = out_spaces or [VMEM] * (len(out_shape) if several else 1)
    return pl.pallas_call(
        kernel,
        out_shape=out_shape,
        in_specs=in_spaces or [VMEM] * len(args),
        out_specs=out_spaces if several else out_spaces[0],
        scratch_shapes=scratch,
        compiler_params=pltpu.CompilerParams(vmem_limit_bytes=mib * 2**20),
        cost_estimate=pl.CostEstimate(flops=flops, bytes_accessed=0, transcendentals=0),
        name=name,
    )(*args)


def exchange(array, axis, within=None):
    return lax.all_to_all(array, axis, split_axis=0, concat_axis=0, tiled=True, axis_index_groups=within)


def per_device(
    hot_table, hot_state, cold_table, cold_state, relation_table, relation_state,
    cold_requests, head_slots, relation_index, tail_slots, negative_slots,
):
    members, groups = lax.axis_size("member"), lax.axis_size("group")
    chips = members // 2
    width = hot_table.shape[1]
    hot, owned, relation_count = hot_table.shape[0], cold_table.shape[0], relation_table.shape[0]
    batch, neg = head_slots.shape[0], negative_slots.shape[1]
    asked = cold_requests.shape[1]
    hot_part, relation_part = hot // members, relation_count // members
    core = lax.axis_index("member") % 2
    same_core = [list(range(k, members, 2)) for k in (0, 1)]
    swap = [(m, m ^ 1) for m in range(members)]

    def place_of(owner, within):
        return ((owner % 2 ^ core) * chips + owner // 2) * BUNDLE + within

    received = exchange(cold_requests.reshape(members, -1), "member")
    cold_half = cold_table.astype(bf16)
    served = call(
        serve_kernel, "serve", shape((asked, width), bf16), (received, cold_half), 61, 2 * asked * owned * width,
        out_spaces=[HBM],
        scratch=[
            pltpu.VMEM((asked, owned), bf16), pltpu.VMEM((asked, width), bf16),
            pltpu.SemaphoreType.DMA((asked // TILE,)),
        ],
    )
    returned = exchange(served.reshape(members, -1, width), "member").reshape(-1, width)

    columns = jnp.stack([head_slots, tail_slots, relation_index, relation_index]).T
    negative_column = negative_slots.reshape(-1, 1)
    slots = jnp.concatenate([head_slots, tail_slots, negative_slots.reshape(-1)])
    places = jnp.where(slots < hot, place_of(slots // hot_part, slots % hot_part), -1).reshape(1, -1)
    slots = slots.reshape(1, -1)
    relation_places = place_of(relation_index // relation_part, hot_part + relation_index % relation_part)

    rows, batch_rows = 2 * batch + neg, shape((batch, width), bf16)
    hot_heads, hot_tails, hot_negatives, relations = call(
        early_kernel, "early", [batch_rows, batch_rows, shape((neg, width), bf16), batch_rows],
        (hot_table.astype(bf16), relation_table.astype(bf16), columns, negative_column), 24,
        2 * rows * hot * width,
    )
    slot_grads, grads, relation_grads, loss = call(
        block_kernel, "block",
        [shape((asked, width), bf16), shape((rows, width), bf16), batch_rows, shape((8, 128), f32)],
        (returned, hot_heads, hot_tails, hot_negatives, relations, columns, negative_column, slots), 61,
        4 * rows * asked * width + 6 * batch * neg * width,
        in_spaces=[HBM] * 7 + [VMEM], out_spaces=[HBM] * 3 + [VMEM],
        scratch=[
            pltpu.VMEM((asked, width), bf16), pltpu.VMEM((batch, width), bf16), pltpu.VMEM((batch, width), bf16),
            pltpu.VMEM((neg, width), bf16), pltpu.VMEM((batch, width), bf16), pltpu.VMEM(columns.shape, jnp.int32),
            pltpu.VMEM((neg, 1), jnp.int32), pltpu.VMEM((rows, width), bf16), pltpu.VMEM((batch, width), bf16),
            pltpu.VMEM((asked, width), bf16), pltpu.VMEM((batch, width), bf16), pltpu.VMEM((batch, neg), bf16),
            pltpu.VMEM((batch, 1), f32), pltpu.VMEM((batch, width), f32), pltpu.SemaphoreType.DMA((7,)),
            pltpu.SemaphoreType.DMA((2 + asked // TILE,)),
        ],
    )
    arrived = exchange(slot_grads.reshape(members, -1, width), "member").reshape(-1, width)

    half, loss_at = chips * BUNDLE, hot_part + relation_part
    mine, other = call(
        functools.partial(shared_kernel, loss_at), "shared",
        [shape((half, width), f32), shape((half, width), bf16)],
        (grads, relation_grads, places, relation_places.reshape(1, -1), loss), 32, 4 * half * (rows + batch) * width,
    )
    other = lax.ppermute(other, "member", swap)
    owner_grad, shared = call(
        owner_kernel, "owner", [shape((owned, width), bf16), shape((half, width), bf16)],
        (received.reshape(1, -1), arrived, mine, other), 24, 2 * asked * owned * width,
    )
    cold_piece = lax.psum_scatter(owner_grad, "group", scatter_dimension=0, tiled=True)
    shared = exchange(shared.reshape(chips, -1, width), "member", same_core)
    shared = call(
        functools.partial(member_sum_kernel, loss_at), "member_sum", shape((groups, BUNDLE, width), bf16), (shared,), 8
    )
    shared, mean_loss = call(
        functools.partial(group_sum_kernel, loss_at, batch * groups * members), "group_sum",
        [shape((members, BUNDLE, width), bf16), shape((8, 128), f32)], (exchange(shared, "group"), cold_piece), 8,
        in_spaces=[VMEM, HBM],
    )
    cold_total = lax.all_gather(cold_piece, "group", axis=0, tiled=True)
    shared = exchange(shared, "member").reshape(-1, width)
    full = lambda *dims: pl.BlockSpec(dims, lambda i: (0,) * len(dims))
    step_rows = pl.BlockSpec((LANES, width), lambda i: (i, 0))
    hot_rows, relation_rows, cold_rows = hot // LANES, relation_count // LANES, owned // LANES
    new_hot_table, new_hot_state, new_relation_table, new_relation_state = pl.pallas_call(
        shared_step_kernel,
        grid=(hot_rows,),
        out_shape=[
            shape((hot, width), f32), shape((hot_rows, LANES), f32),
            shape((relation_count, width), f32), shape((relation_rows, LANES), f32),
        ],
        in_specs=[
            full(*shared.shape), step_rows, full(hot_rows, LANES), full(relation_count, width), full(relation_rows, LANES),
        ],
        out_specs=[step_rows, full(hot_rows, LANES), full(relation_count, width), full(relation_rows, LANES)],
        scratch_shapes=[pltpu.VMEM((hot, width), f32)],
        compiler_params=pltpu.CompilerParams(vmem_limit_bytes=20 * 2**20),
        name="shared_step",
    )(shared, hot_table, hot_state.reshape(-1, LANES), relation_table, relation_state.reshape(-1, LANES))
    new_cold_table, new_cold_state = pl.pallas_call(
        cold_step_kernel,
        grid=(cold_rows,),
        out_shape=[shape((owned, width), f32), shape((cold_rows, LANES), f32)],
        in_specs=[step_rows, step_rows, full(cold_rows, LANES)],
        out_specs=[step_rows, full(cold_rows, LANES)],
        compiler_params=pltpu.CompilerParams(vmem_limit_bytes=12 * 2**20),
        name="cold_step",
    )(cold_total, cold_table, cold_state.reshape(-1, LANES))
    return (
        new_hot_table, new_hot_state.reshape(-1), new_cold_table, new_cold_state.reshape(-1),
        new_relation_table, new_relation_state.reshape(-1), mean_loss[0, 0],
    )


def solution(mesh):
    placed = (
        P(), P(), P("member", None), P("member"), P(), P(), P(("group", "member"), None),
        P(("group", "member")), P(("group", "member")), P(("group", "member")), P(("group", "member"), None),
    )
    return jax.shard_map(
        per_device, mesh=mesh, in_specs=placed,
        out_specs=(P(), P(), P("member", None), P("member"), P(), P(), P()), check_vma=False,
    )
```

time: 315 us -> 244 us (0.77)
  waiting for transfers between devices: 127 us -> 63.1 us
  other arithmetic: 27 us -> 6.41 us
  local copies, waits for them, and re-layouts: 14.6 us -> 23.9 us
  between operations: 6.31 us -> 14.4 us
  starting transfers between devices: 34.2 us -> 28.4 us
    all_to_all x6 -> x4, waiting for transfers between devices: 127 us -> 22.7 us  [exchange(): lax.all_to_all(array, axis, split_axis=0, concat_axis=0, tiled=True, axis...]
    all_gather x0 -> x1, waiting for transfers between devices: none -> 37.8 us  [per_device(): cold_total = lax.all_gather(cold_piece, 'group', axis=0, tiled=True)]
    unnamed x31 -> x61, local copies, waits for them, and re-layouts: 9.48 us -> 21.5 us
    reduce_sum x8 -> x0, other arithmetic: 11.6 us -> none  [the longest x3 6.92 us: adagrad(): new_state = acc_state + jnp.mean(row_grad * row_grad, -1)]
    sub x3 -> x0, other arithmetic: 9.64 us -> none  [adagrad(): emb_table - learn_rate * row_grad / jnp.sqrt(new_state)[:, None]]
    all_to_all x6 -> x4, starting transfers between devices: 34.2 us -> 28.2 us  [exchange(): lax.all_to_all(array, axis, split_axis=0, concat_axis=0, tiled=True, axis...]
    broadcast_in_dim x3 -> x0, local copies, waits for them, and re-layouts: 3.61 us -> none  [the longest x1 1.66 us: per_device(): jnp.broadcast_to(shared[None], (members,) + shared.shape)]
    convert_element_type x3, other arithmetic: 0.55 us -> 4.15 us  [the longest x1 2.73 us: per_device(): cold_half = cold_table.astype(bf16)]
  transfers between devices with their start and end apart: 6 -> 7, of which waited for: 6 -> 5; matrix products, arithmetic and copies ran while one was open for 6% -> 3% of each run, Pallas kernels for 1% -> 7%
where the time goes in v2:
time: 244 us; the launch traced here: 243 us
  waiting for transfers between devices  63.1 us (26%)
  Pallas kernels  59.8 us (25%)
  blocking collectives  47.1 us (19%)
  starting transfers between devices  28.4 us (12%)
  local copies, waits for them, and re-layouts  23.9 us (10%)
  between operations  14.4 us (6%)
  other arithmetic  6.41 us (3%)
    pallas_call x7, Pallas kernels, call(): pl.pallas_call(kernel, out_shape=out_shape, in_specs=in_spaces or [VMEM]...  52.3 us
    all_to_all x2, blocking collectives, exchange(): lax.all_to_all(array, axis, split_axis=0, concat_axis=0, tiled=True, axis...  47.1 us
    all_gather x1, waiting for transfers between devices, per_device(): cold_total = lax.all_gather(cold_piece, 'group', axis=0, tiled=True)  37.8 us
    all_to_all x4, starting transfers between devices, exchange(): lax.all_to_all(array, axis, split_axis=0, concat_axis=0, tiled=True, axis...  28.2 us
    all_to_all x4, waiting for transfers between devices, exchange(): lax.all_to_all(array, axis, split_axis=0, concat_axis=0, tiled=True, axis...  22.7 us
    unnamed x61, local copies, waits for them, and re-layouts  21.5 us
    pallas_call x1, Pallas kernels, per_device(): pl.pallas_call(shared_step_kernel, grid=(hot_rows,), out_shape=[shape((ho...  5.28 us
  transfers between devices with their start and end apart: 7, of which 5 were waited for; matrix products, arithmetic and copies ran while one was open for 3% of the time, Pallas kernels for 7%

profile of v2, /device:TPU:2, one launch (start us, length us, event | category | flops | bytes accessed | tf_op | source)
XLA Modules:
  0.0 243.1 jit_solution(17933796295547755310)
XLA Ops:
  7.2 0.5 broadcast.190
  7.7 1.3 reduce.6
  9.0 0.7 all_to_all.22
  9.7 7.6 %all-to-all-start = ((s32[32,1,32]{2,1,0:T(1,128)}), s32[32,1,32]{2,1,0:T(1,128)S(1)}, u32[]{:S(2)}, u32[]{:S(2)}) async-start(s32[32,1,32]{2,1,0:T(1,128)} %all_to_all.22), calls=%async_computation | async-start | bytes 32768 | tf_op jit(solution)/shard_map/all_to_all | solution.py:286
  17.3 2.7 %convert_element_type.9.half_ref = bf16[512,1024]{1,0:T(8,128)(2,1)} convert(f32[512,1024]{1,0:T(8,128)} %table_ref.1) | non-fusion elementwise | flops 524288 | bytes 3145728 | tf_op jit(solution)/shard_map/convert_element_type | solution.py:308
  20.1 3.4 %all-to-all-done = s32[32,1,32]{2,1,0:T(1,128)S(1)} async-done(((s32[32,1,32]{2,1,0:T(1,128)}), s32[32,1,32]{2,1,0:T(1,128)S(1)}, u32[]{:S(2)}, u32[]{:S(2)}) %all-to-all-start) | async-done | bytes 4128 | tf_op jit(solution)/shard_map/all_to_all | solution.py:286
  23.5 0.6 copy-done.24
  24.1 3.5 %serve.1 = bf16[1024,1024]{1,0:T(8,128)(2,1)} custom-call(s32[32,32]{1,0:T(8,128)} %bitcast.30, bf16[512,1024]{1,0:T(8,128)(2,1)} %convert_element_type.9.half_ref), custom_call_target="tpu_custom_call" | custom-call | flops 1073741824 | tf_op jit(solution)/shard_map/serve/pallas_call | solution.py:273
  27.6 6.1 %all-to-all-start.1 = ((bf16[32,32,1024]{2,1,0:T(8,128)(2,1)}), bf16[32,32,1024]{2,1,0:T(8,128)(2,1)}, u32[]{:S(2)}, u32[]{:S(2)}) async-start(bf16[32,32,1024]{2,1,0:T(8,128)(2,1)} %bitcast.28), calls=%async_computation.1 | async-start | bytes 4194304 | tf_op jit(solution)/shard_map/all_to_all | solution.py:286
  33.8 1.4 convert_element_type.10.hot_ref
  35.3 0.2 copy.24.columns_ref.columns_hbm
  35.7 0.7 reshape.333.slots_ref
  36.4 1.4 copy-done.7
  37.8 5.3 %early.1 = (bf16[1024,1024]{1,0:T(8,128)(2,1)S(1)}, bf16[1024,1024]{1,0:T(8,128)(2,1)S(1)}, bf16[512,1024]{1,0:T(8,128)(2,1)S(1)}, bf16[1024,1024]{1,0:T(8,128)(2,1)S(1)}) custom-call(bf16[768,1024]{1,0:T(8,128)(2,1)S(1)} %copy-done.7, bf16[128,1024]{1,0:T(8,128)(2,1)S(1)} %convert_element_type.11.relation_ref, s32[1024,4]{1,0:T(8,128)S(1)} %copy.24.columns_ref.columns_hbm, ...), custom_call_target="tpu_custom_call" | custom-call | flops 4026531840 | tf_op jit(solution)/shard_map/early/pallas_call | solution.py:273
  43.2 1.3 copy-done.17
  44.5 1.4 copy-done.18
  45.8 1.3 copy-done.19
  47.2 1.0 copy-done.21
  48.1 11.6 %all-to-all-done.1 = bf16[32,32,1024]{2,1,0:T(8,128)(2,1)} async-done(((bf16[32,32,1024]{2,1,0:T(8,128)(2,1)}), bf16[32,32,1024]{2,1,0:T(8,128)(2,1)}, u32[]{:S(2)}, u32[]{:S(2)}) %all-to-all-start.1) | async-done | bytes 2097184 | tf_op jit(solution)/shard_map/all_to_all | solution.py:286
  59.7 30.5 %block.1 = (bf16[1024,1024]{1,0:T(8,128)(2,1)}, bf16[2560,1024]{1,0:T(8,128)(2,1)}, bf16[1024,1024]{1,0:T(8,128)(2,1)}, f32[8,128]{1,0:T(8,128)}) custom-call(bf16[1024,1024]{1,0:T(8,128)(2,1)} %bitcast.2.cold_hbm, bf16[1024,1024]{1,0:T(8,128)(2,1)} %copy-done.17, bf16[1024,1024]{1,0:T(8,128)(2,1)} %copy-done.18, bf16[512,1024]{1,0:T(8,128)(2,1)} %copy-done.21, ...), custom_call_target="tpu_custom_call" | custom-call | flops 13958643712 | tf_op jit(solution)/shard_map/block/pallas_call | solution.py:273
  90.2 7.2 %all-to-all-start.2 = ((bf16[32,32,1024]{2,1,0:T(8,128)(2,1)}), bf16[32,32,1024]{2,1,0:T(8,128)(2,1)S(1)}, u32[]{:S(2)}, u32[]{:S(2)}) async-start(bf16[32,32,1024]{2,1,0:T(8,128)(2,1)} %bitcast.29), calls=%async_computation.2 | async-start | bytes 4194304 | tf_op jit(solution)/shard_map/all_to_all | solution.py:286
  97.4 0.2 compare_select_fusion.places_ref
  97.6 2.5 %copy-done.20 = bf16[2560,1024]{1,0:T(8,128)(2,1)S(1)} copy-done((bf16[2560,1024]{1,0:T(8,128)(2,1)S(1)}, bf16[2560,1024]{1,0:T(8,128)(2,1)}, u32[]{:S(2)}) %copy-start.20) | copy-done | bytes 5242904
  100.1 1.6 copy-done.22
  101.7 8.7 %shared.1 = (f32[512,1024]{1,0:T(8,128)S(1)}, bf16[512,1024]{1,0:T(8,128)(2,1)}) custom-call(bf16[2560,1024]{1,0:T(8,128)(2,1)S(1)} %copy-done.20, bf16[1024,1024]{1,0:T(8,128)(2,1)S(1)} %copy-done.22, s32[1,2560]{1,0:T(1,128)S(1)} %compare_select_fusion.places_ref, s32[1,1024]{1,0:T(1,128)S(1)} %bitcast.24, f32[8,128]{1,0:T(8,128)S(1)} %copy-done.23), custom_call_target="tpu_custom_call" | custom-call | flops 7516192768 | tf_op jit(solution)/shard_map/shared/pallas_call | solution.py:273
  110.4 1.3 copy-done.3
  111.7 0.1 collective-permute-start
  111.9 0.7 reduce.7
  112.7 1.9 collective-permute-done.other_ref
  114.6 1.0 copy-done.8
  115.6 7.7 %all-to-all-done.2 = bf16[32,32,1024]{2,1,0:T(8,128)(2,1)S(1)} async-done(((bf16[32,32,1024]{2,1,0:T(8,128)(2,1)}), bf16[32,32,1024]{2,1,0:T(8,128)(2,1)S(1)}, u32[]{:S(2)}, u32[]{:S(2)}) %all-to-all-start.2) | async-done | bytes 2097184 | tf_op jit(solution)/shard_map/all_to_all | solution.py:286
  123.3 1.6 copy-done.4
  124.9 1.2 copy-done.9
  126.1 2.6 %owner.1 = (bf16[512,1024]{1,0:T(8,128)(2,1)}, bf16[512,1024]{1,0:T(8,128)(2,1)S(1)}) custom-call(s32[1,1024]{1,0:T(1,128)S(1)} %reshape.328.row_ref, bf16[1024,1024]{1,0:T(8,128)(2,1)S(1)} %bitcast.22, f32[512,1024]{1,0:T(8,128)S(1)} %copy-done.4, bf16[512,1024]{1,0:T(8,128)(2,1)S(1)} %copy-done.9), custom_call_target="tpu_custom_call" | custom-call | flops 1073741824 | tf_op jit(solution)/shard_map/owner/pallas_call | solution.py:273
  128.7 21.0 %all_to_all.36.parts_ref = bf16[16,32,1024]{2,1,0:T(8,128)(2,1)S(1)} all-to-all(bf16[16,32,1024]{2,1,0:T(8,128)(2,1)S(1)} %bitcast.23), channel_id=1, replica_groups={{0,2,4,6,8,10,12,14,16,18,20,22,24,26,28,30},{1,3,5,7,9,11,13,15,17,19,..., dimensions={0} | all-to-all | bytes 2097152 | tf_op jit(solution)/shard_map/all_to_all | solution.py:286
  149.7 0.2 member_sum.1
  149.9 26.1 %all_to_all.37.parts_ref = bf16[8,32,1024]{2,1,0:T(8,128)(2,1)S(1)} all-to-all(bf16[8,32,1024]{2,1,0:T(8,128)(2,1)S(1)} %member_sum.1), channel_id=1, replica_groups=mesh['group'=8,'member'=32] {'group'}, dimensions={0} | all-to-all | bytes 1048576 | tf_op jit(solution)/shard_map/all_to_all | solution.py:286
  176.0 0.9 copy-done.11
  176.9 1.5 group_sum.1
  178.5 7.3 %all-to-all-start.5 = ((bf16[32,32,1024]{2,1,0:T(8,128)(2,1)}), bf16[32,32,1024]{2,1,0:T(8,128)(2,1)}, u32[]{:S(2)}, u32[]{:S(2)}) async-start(bf16[32,32,1024]{2,1,0:T(8,128)(2,1)} %get-tuple-element.39), calls=%async_computation.6 | async-start | bytes 4194304 | tf_op jit(solution)/shard_map/all_to_all | solution.py:286
  185.9 0.7 all-gather.2.cloned.1.call-update
  186.6 0.5 slice.3
  187.1 37.8 %all-gather.2.cloned.1.call-done.grad_ref = bf16[512,1024]{1,0:T(8,128)(2,1)} async-done(((bf16[64,1024]{1,0:T(8,128)(2,1)}), bf16[512,1024]{1,0:T(8,128)(2,1)}) %all-gather.2.cloned.1.call-update) | async-done | bytes 1048592 | tf_op jit(solution)/shard_map/all_gather | solution.py:370
  224.9 1.6 copy-done.2
  226.5 1.2 copy-done.10
  227.7 2.2 cold_step.1
  229.9 1.0 copy-done.6
  231.0 5.3 %shared_step.1 = (f32[768,1024]{1,0:T(8,128)}, f32[6,128]{1,0:T(8,128)}, f32[128,1024]{1,0:T(8,128)}, f32[1,128]{1,0:T(1,128)}) custom-call(bf16[1024,1024]{1,0:T(8,128)(2,1)} %bitcast.13.shared_ref, f32[768,1024]{1,0:T(8,128)S(1)} %copy-done.1, f32[6,128]{1,0:T(8,128)S(1)} %bitcast.25, f32[128,1024]{1,0:T(8,128)S(1)} %copy-done.6, f32[1,128]{1,0:T(1,128)S(1)} %bitcast.27), custom_call_target="tpu_custom_call" | custom-call | tf_op jit(solution)/shard_map/shared_step/pallas_call | solution.py:375
  (55 shorter events, 0.5 us)
Async XLA Ops:
  9.7 13.7 %all-to-all-start = ((s32[32,1,32]{2,1,0:T(1,128)}), s32[32,1,32]{2,1,0:T(1,128)S(1)}, u32[]{:S(2)}, u32[]{:S(2)}) async-start(s32[32,1,32]{2,1,0:T(1,128)} %all_to_all.22), calls=%async_computation | async-start | bytes 32768 | tf_op jit(solution)/shard_map/all_to_all | solution.py:286
  23.5 0.6 copy-start.24
  27.6 6.1 %copy-start = (f32[768,1024]{1,0:T(8,128)S(1)}, f32[768,1024]{1,0:T(8,128)}, u32[]{:S(2)}) copy-start(f32[768,1024]{1,0:T(8,128)} %hot_ref.1) | copy-start | bytes 9437188
  27.6 32.1 %all-to-all-start.1 = ((bf16[32,32,1024]{2,1,0:T(8,128)(2,1)}), bf16[32,32,1024]{2,1,0:T(8,128)(2,1)}, u32[]{:S(2)}, u32[]{:S(2)}) async-start(bf16[32,32,1024]{2,1,0:T(8,128)(2,1)} %bitcast.28), calls=%async_computation.1 | async-start | bytes 4194304 | tf_op jit(solution)/shard_map/all_to_all | solution.py:286
  33.7 1.5 copy-start.5
  33.7 1.5 copy-start.26
  33.7 1.5 copy-start.27
  33.8 1.5 copy-start.29
  33.8 1.7 copy-start.28
  35.5 7.6 %copy-start.12 = (s32[1024,4]{1,0:T(8,128)}, s32[1024,4]{1,0:T(8,128)S(1)}, u32[]{:S(2)}) copy-start(s32[1024,4]{1,0:T(8,128)S(1)} %copy.24.columns_ref.columns_hbm) | copy-start | bytes 49156
  35.7 7.5 %copy-start.13 = (s32[512,1]{1,0:T(8,128)}, s32[512,1]{1,0:T(8,128)S(1)}, u32[]{:S(2)}) copy-start(s32[512,1]{1,0:T(8,128)S(1)} %copy.25.negative_column_ref.negative_column_hbm) | copy-start | bytes 6148
  36.4 1.4 copy-start.7
  43.1 1.3 copy-start.17
  44.5 1.4 copy-start.18
  45.8 1.3 copy-start.19
  47.2 1.0 copy-start.21
  90.2 7.4 %copy-start.23 = (f32[8,128]{1,0:T(8,128)S(1)}, f32[8,128]{1,0:T(8,128)}, u32[]{:S(2)}) copy-start(f32[8,128]{1,0:T(8,128)} %get-tuple-element.34.loss_ref) | copy-start | bytes 12292
  90.2 33.1 %all-to-all-start.2 = ((bf16[32,32,1024]{2,1,0:T(8,128)(2,1)}), bf16[32,32,1024]{2,1,0:T(8,128)(2,1)S(1)}, u32[]{:S(2)}, u32[]{:S(2)}) async-start(bf16[32,32,1024]{2,1,0:T(8,128)(2,1)} %bitcast.29), calls=%async_computation.2 | async-start | bytes 4194304 | tf_op jit(solution)/shard_map/all_to_all | solution.py:286
  97.4 78.7 %reduce-scatter.2.cloned.1.call-start = ((), (), s32[]{:S(2)}) async-start(), calls=%async_computation.7 | async-start | bytes 1179648 | tf_op jit(solution)/shard_map/reduce_scatter | solution.py:360
  97.6 2.5 %copy-start.20 = (bf16[2560,1024]{1,0:T(8,128)(2,1)S(1)}, bf16[2560,1024]{1,0:T(8,128)(2,1)}, u32[]{:S(2)}) copy-start(bf16[2560,1024]{1,0:T(8,128)(2,1)} %get-tuple-element.32.grads_ref) | copy-start | bytes 15728644
  100.1 1.6 copy-start.22
  101.7 10.2 %copy-start.25 = (s32[32,1,32]{2,1,0:T(1,128)S(1)}, s32[32,1,32]{2,1,0:T(1,128)}, u32[]{:S(2)}) copy-start(s32[32,1,32]{2,1,0:T(1,128)} %copy-done.24) | copy-start | bytes 12292
  110.4 1.3 copy-start.3
  111.7 2.9 %collective-permute-start = (bf16[512,1024]{1,0:T(8,128)(2,1)}, bf16[512,1024]{1,0:T(8,128)(2,1)S(1)}, u32[]{:S(2)}, u32[]{:S(2)}) collective-permute-start(bf16[512,1024]{1,0:T(8,128)(2,1)} %get-tuple-element.36), channel_id=1, source_target_pairs={{0,1},{1,0},{2,3},{3,2},{4,5},{5,4},{6,7},{7,6},{8,9},{9,8},{10,11... | collective-permute-start | bytes 3145736 | tf_op jit(solution)/shard_map/ppermute | solution.py:355
  114.6 1.0 copy-start.8
  123.3 1.6 copy-start.4
  124.9 1.2 copy-start.9
  176.0 0.9 copy-start.11
  178.5 46.4 %copy-start.15 = (f32[512]{0:T(512)S(1)}, f32[512]{0:T(512)}, u32[]{:S(2)}) copy-start(f32[512]{0:T(512)} %param.14) | copy-start | bytes 6148
  178.5 51.4 %copy-start.14 = (f32[768]{0:T(1024)S(1)}, f32[768]{0:T(1024)}, u32[]{:S(2)}) copy-start(f32[768]{0:T(1024)} %param.12) | copy-start | bytes 9220
  178.5 51.4 %copy-start.16 = (f32[128]{0:T(128)S(1)}, f32[128]{0:T(128)}, u32[]{:S(2)}) copy-start(f32[128]{0:T(128)} %param.16) | copy-start | bytes 1540
  178.5 51.4 %all-to-all-start.5 = ((bf16[32,32,1024]{2,1,0:T(8,128)(2,1)}), bf16[32,32,1024]{2,1,0:T(8,128)(2,1)}, u32[]{:S(2)}, u32[]{:S(2)}) async-start(bf16[32,32,1024]{2,1,0:T(8,128)(2,1)} %get-tuple-element.39), calls=%async_computation.6 | async-start | bytes 4194304 | tf_op jit(solution)/shard_map/all_to_all | solution.py:286
  185.8 44.1 %copy-start.1 = (f32[768,1024]{1,0:T(8,128)S(1)}, f32[768,1024]{1,0:T(8,128)}, u32[]{:S(2)}) copy-start(f32[768,1024]{1,0:T(8,128)} %hot_ref.1) | copy-start | bytes 9437188
  185.8 39.1 %all-gather.2.cloned.1.call-start = ((), (), s32[]{:S(2)}) async-start(), calls=%async_computation.8 | async-start | bytes 1179648 | tf_op jit(solution)/shard_map/all_gather | solution.py:370
  224.9 1.6 copy-start.2
  226.5 1.2 copy-start.10
  229.9 1.0 copy-start.6
Sparse Core Ops, SparseCore 0:
  128.8 43.8 reduce-scatter.1
  188.5 36.3 all-gather.1

commit v3 on v2

--- a/solution.py
+++ b/solution.py
@@ -15,6 +15,7 @@
 LANES = 128
 VMEM = pl.BlockSpec(memory_space=pltpu.VMEM)
 HBM = pl.BlockSpec(memory_space=pltpu.HBM)
+SMEM = pl.BlockSpec(memory_space=pltpu.SMEM)
 shape = jax.ShapeDtypeStruct
 
 
@@ -52,15 +53,20 @@
     return jnp.sum(jnp.where(diagonal(column.shape[0]), column, 0.0), 0, keepdims=True)
 
 
+def requests_kernel(wanted_ref, out_ref):
+    members, _, slots = out_ref.shape
+    for member in range(members):
+        out_ref[member] = wanted_ref[:, member * slots : (member + 1) * slots]
+
+
 def serve_kernel(received_ref, half_ref, out_ref, hits, rows_out, sems):
-    members, slots = received_ref.shape
+    members, _, slots = received_ref.shape
     owned = half_ref.shape[0]
     ids = lax.broadcasted_iota(jnp.int32, (slots, owned), 1).astype(f32)
-    received = received_ref[...].astype(f32)
     copies = []
     for first in range(0, members * slots, TILE):
         for member in range(first // slots, (first + TILE) // slots):
-            column = to_column(received[member : member + 1, :])
+            column = to_column(received_ref[member].astype(f32))
             hits[member * slots : (member + 1) * slots, :] = jnp.where(column == ids, 1.0, 0.0).astype(bf16)
         rows = pl.ds(first, TILE)
         rows_out[rows, :] = dot(hits[rows, :], half_ref[...]).astype(bf16)
@@ -211,13 +217,24 @@
     return sum((part.astype(f32) for part in parts[1:]), parts[0].astype(f32))
 
 
-def owner_kernel(row_ref, arrived_ref, mine_ref, other_ref, owner_ref, shared_ref):
+def chip_sum_kernel(mine_ref, other_ref, shared_ref):
     shared_ref[...] = (mine_ref[...] + other_ref[...].astype(f32)).astype(bf16)
-    hits = spread_rows(row_ref[...], row_ids(0, owner_ref.shape[0], 1))
-    owner_ref[...] = dot(hits, arrived_ref[...]).astype(bf16)
-
-
-def member_sum_kernel(loss_at, parts_ref, out_ref):
+
+
+def owner_kernel(group_ref, row_ref, arrived_ref, _shared, _same, *out_refs):
+    groups, piece = len(out_refs), out_refs[0].shape[0]
+    total = row_ids(0, groups * piece, 1)
+    ids = (total // piece + group_ref[0]) % groups * piece + total % piece
+    found = dot(spread_rows(row_ref[...], ids), arrived_ref[...])
+    for k, out_ref in enumerate(out_refs):
+        out_ref[...] = found[k * piece : (k + 1) * piece, :].astype(bf16)
+
+
+def cold_sum_kernel(*refs):
+    refs[-1][...] = total_of([ref[...] for ref in refs[:-1]]).astype(bf16)
+
+
+def member_sum_kernel(loss_at, parts_ref, _after, out_ref):
     total = total_of([parts_ref[k] for k in range(parts_ref.shape[0])])
     loss = jnp.sum(total[loss_at : loss_at + 1, :], -1, keepdims=True)
     total = jnp.where(row_ids(0, BUNDLE, 1) == loss_at, loss_pieces(loss, total.shape[1]), total).astype(bf16)
@@ -225,7 +242,8 @@
         out_ref[k] = total
 
 
-def group_sum_kernel(loss_at, batch_total, parts_ref, _after, shared_ref, loss_ref):
+def group_sum_kernel(loss_at, batch_total, parts_ref, *refs):
+    shared_ref, loss_ref = refs[-2:]
     total = total_of([parts_ref[k] for k in range(parts_ref.shape[0])])
     loss = jnp.sum(total[loss_at : loss_at + 1, :], -1, keepdims=True)
     loss_ref[...] = jnp.broadcast_to(loss / batch_total, loss_ref.shape)
@@ -236,38 +254,71 @@
 
 def stepped(table, state_row, grad):
     new_state = to_column(state_row) + jnp.mean(grad * grad, -1, keepdims=True)
-    return table - learn_rate * grad / jnp.sqrt(new_state), to_row(new_state)
-
-
-def cold_step_kernel(grad_ref, table_ref, state_ref, new_table, new_state):
-    at_row = pl.ds(pl.program_id(0), 1)
-    new_table[...], new_state[at_row, :] = stepped(table_ref[...], state_ref[at_row, :], grad_ref[...].astype(f32))
+    return table - grad * (learn_rate / jnp.sqrt(new_state)), to_row(new_state)
+
+
+def stream_steps(jobs, sems_in, sems_out):
+    blocks = [(job, k) for job in jobs for k in range(job[1].shape[0] // LANES)]
+    part = lambda k: pl.ds(k * LANES, LANES)
+    loads = [
+        pltpu.make_async_copy(job[0].at[part(k)], job[1].at[part(k)], sems_in.at[n]) for n, (job, k) in enumerate(blocks)
+    ]
+    stores = [
+        pltpu.make_async_copy(job[5].at[part(k)], job[4].at[part(k)], sems_out.at[n]) for n, (job, k) in enumerate(blocks)
+    ]
+    for load in loads:
+        load.start()
+
+    def run():
+        for load, store, (job, k) in zip(loads, stores, blocks):
+            _, table, state, grad, _, result, new_state = job
+            load.wait()
+            result[part(k), :], new_state[k : k + 1, :] = stepped(
+                table[part(k), :], state[k : k + 1, :], grad[part(k), :].astype(f32)
+            )
+            store.start()
+        for store in stores:
+            store.wait()
+
+    return run
+
+
+def cold_step_kernel(group_ref, table_hbm, state_ref, *refs):
+    pieces, (new_table, new_state, table, result, grads, sems_in, sems_out) = refs[:-7], refs[-7:]
+    run = stream_steps([(table_hbm, table, state_ref, grads, new_table, result, new_state)], sems_in, sems_out)
+    groups, piece = len(pieces), pieces[0].shape[0]
+    for k, piece_ref in enumerate(pieces):
+        grads[at(lax.rem(group_ref[0] + groups - k, groups), piece), :] = piece_ref[...]
+    run()
 
 
 def shared_step_kernel(
-    shared_ref, hot_ref, hot_state_ref, relation_ref, relation_state_ref,
-    new_hot, new_hot_state, new_relation, new_relation_state, grads,
+    core_ref, mine_ref, other_ref, hot_hbm, hot_state, relation_hbm, relation_state, new_hot, new_hot_state, new_relation, new_relation_state,
+    hot_table, hot_result, hot_grads, relation_table, relation_result, relation_grads, sems_in, sems_out,
 ):
-    step = pl.program_id(0)
-
-    @pl.when(step == 0)
-    def _():
-        members = shared_ref.shape[0] // BUNDLE
-        hot_part, relation_part = grads.shape[0] // members, relation_ref.shape[0] // members
-        relation_grad = []
-        for member in range(members):
-            bundle = shared_ref[member * BUNDLE : (member + 1) * BUNDLE, :].astype(f32)
-            grads[member * hot_part : (member + 1) * hot_part, :] = bundle[:hot_part, :]
-            relation_grad.append(bundle[hot_part : hot_part + relation_part, :])
-        new_relation[...], new_relation_state[...] = stepped(
-            relation_ref[...], relation_state_ref[...], jnp.concatenate(relation_grad)
+    run = stream_steps(
+        [
+            (hot_hbm, hot_table, hot_state, hot_grads, new_hot, hot_result, new_hot_state),
+            (relation_hbm, relation_table, relation_state, relation_grads, new_relation, relation_result, new_relation_state),
+        ],
+        sems_in, sems_out,
+    )
+    members = 2 * mine_ref.shape[0] // BUNDLE
+    hot_part, relation_part = hot_grads.shape[0] // members, relation_grads.shape[0] // members
+    first = core_ref[0] == 0
+    for member in range(0, members, 2):
+        rows = slice(member // 2 * BUNDLE, (member // 2 + 1) * BUNDLE)
+        mine, other = mine_ref[rows, :].astype(f32), other_ref[rows, :].astype(f32)
+        pair = (jnp.where(first, mine, other), jnp.where(first, other, mine))
+        for k, grad in enumerate(pair):
+            hot_grads[(member + k) * hot_part : (member + k + 1) * hot_part, :] = grad[:hot_part, :]
+        relation_grads[member * relation_part : (member + 2) * relation_part, :] = jnp.concatenate(
+            [grad[hot_part : hot_part + relation_part, :] for grad in pair]
         )
-
-    at_row = pl.ds(step, 1)
-    new_hot[...], new_hot_state[at_row, :] = stepped(hot_ref[...], hot_state_ref[at_row, :], grads[at(step, LANES), :])
-
-
-def call(kernel, name, out_shape, args, mib, flops=0, in_spaces=None, out_spaces=None, scratch=()):
+    run()
+
+
+def call(kernel, name, out_shape, args, mib, flops=0, in_spaces=None, out_spaces=None, scratch=(), aliases=None):
     several = isinstance(out_shape, list)
     out_spaces = out_spaces or [VMEM] * (len(out_shape) if several else 1)
     return pl.pallas_call(
@@ -276,6 +327,7 @@
         in_specs=in_spaces or [VMEM] * len(args),
         out_specs=out_spaces if several else out_spaces[0],
         scratch_shapes=scratch,
+        input_output_aliases=aliases or {},
         compiler_params=pltpu.CompilerParams(vmem_limit_bytes=mib * 2**20),
         cost_estimate=pl.CostEstimate(flops=flops, bytes_accessed=0, transcendentals=0),
         name=name,
@@ -298,13 +350,15 @@
     asked = cold_requests.shape[1]
     hot_part, relation_part = hot // members, relation_count // members
     core = lax.axis_index("member") % 2
+    group_at, core_at = lax.axis_index("group").reshape(1), core.reshape(1)
     same_core = [list(range(k, members, 2)) for k in (0, 1)]
     swap = [(m, m ^ 1) for m in range(members)]
 
     def place_of(owner, within):
         return ((owner % 2 ^ core) * chips + owner // 2) * BUNDLE + within
 
-    received = exchange(cold_requests.reshape(members, -1), "member")
+    wanted = call(requests_kernel, "requests", shape((members, 1, asked // members), jnp.int32), (cold_requests,), 61)
+    received = exchange(wanted, "member")
     cold_half = cold_table.astype(bf16)
     served = call(
         serve_kernel, "serve", shape((asked, width), bf16), (received, cold_half), 61, 2 * asked * owned * width,
@@ -353,49 +407,56 @@
         (grads, relation_grads, places, relation_places.reshape(1, -1), loss), 32, 4 * half * (rows + batch) * width,
     )
     other = lax.ppermute(other, "member", swap)
-    owner_grad, shared = call(
-        owner_kernel, "owner", [shape((owned, width), bf16), shape((half, width), bf16)],
-        (received.reshape(1, -1), arrived, mine, other), 24, 2 * asked * owned * width,
-    )
-    cold_piece = lax.psum_scatter(owner_grad, "group", scatter_dimension=0, tiled=True)
+    shared = call(chip_sum_kernel, "chip_sum", shape((half, width), bf16), (mine, other), 8)
+    piece = owned // groups
+    shared, *pieces = call(
+        owner_kernel, "owner", [shape((half, width), bf16)] + [shape((piece, width), bf16)] * groups,
+        (group_at, received.reshape(1, -1), arrived, shared), 24, 2 * asked * owned * width,
+        in_spaces=[SMEM, VMEM, VMEM, HBM], out_spaces=[HBM] + [VMEM] * groups, aliases={3: 0},
+    )
+    ways = [(k, [(g, (g + k) % groups) for g in range(groups)]) for k in range(1, groups)]
+    pieces = [pieces[0]] + [lax.ppermute(pieces[k], "group", way) for k, way in ways]
+    cold_piece = call(cold_sum_kernel, "cold_sum", shape((piece, width), bf16), pieces, 8)
+
     shared = exchange(shared.reshape(chips, -1, width), "member", same_core)
     shared = call(
-        functools.partial(member_sum_kernel, loss_at), "member_sum", shape((groups, BUNDLE, width), bf16), (shared,), 8
-    )
+        functools.partial(member_sum_kernel, loss_at), "member_sum", shape((groups, BUNDLE, width), bf16),
+        (shared, cold_piece), 8, in_spaces=[VMEM, HBM],
+    )
+    sent = {k: lax.ppermute(cold_piece, "group", way) for k, way in ways}
+    near, far = [sent[k] for k in (1, 7, 2, 6)], [sent[k] for k in (3, 5, 4)]
     shared, mean_loss = call(
         functools.partial(group_sum_kernel, loss_at, batch * groups * members), "group_sum",
-        [shape((members, BUNDLE, width), bf16), shape((8, 128), f32)], (exchange(shared, "group"), cold_piece), 8,
-        in_spaces=[VMEM, HBM],
-    )
-    cold_total = lax.all_gather(cold_piece, "group", axis=0, tiled=True)
-    shared = exchange(shared, "member").reshape(-1, width)
-    full = lambda *dims: pl.BlockSpec(dims, lambda i: (0,) * len(dims))
-    step_rows = pl.BlockSpec((LANES, width), lambda i: (i, 0))
-    hot_rows, relation_rows, cold_rows = hot // LANES, relation_count // LANES, owned // LANES
-    new_hot_table, new_hot_state, new_relation_table, new_relation_state = pl.pallas_call(
-        shared_step_kernel,
-        grid=(hot_rows,),
-        out_shape=[
-            shape((hot, width), f32), shape((hot_rows, LANES), f32),
-            shape((relation_count, width), f32), shape((relation_rows, LANES), f32),
+        [shape((chips, BUNDLE, width), bf16), shape((8, 128), f32)], (exchange(shared, "group"), *near), 8,
+        in_spaces=[VMEM] + [HBM] * len(near),
+    )
+    pieces = [cold_piece] + [sent[k] for k in range(1, groups)]
+    mine = exchange(shared, "member", same_core).reshape(-1, width)
+    mine = call(
+        lambda *refs: None, "after_far", shape(mine.shape, bf16), (mine, *far), 8,
+        in_spaces=[HBM] * (1 + len(far)), out_spaces=[HBM], aliases={0: 0},
+    )
+    other = lax.ppermute(mine, "member", swap)
+    state = lambda array: array.reshape(-1, LANES)
+    buffers = lambda count: [pltpu.VMEM((count, width), f32), pltpu.VMEM((count, width), f32)]
+    sems = lambda count: [pltpu.SemaphoreType.DMA((count // LANES,))] * 2
+    new_cold_table, new_cold_state = call(
+        cold_step_kernel, "cold_step", [shape((owned, width), f32), shape((owned // LANES, LANES), f32)],
+        (group_at, cold_table, state(cold_state), *pieces), 61,
+        in_spaces=[SMEM, HBM] + [VMEM] * (groups + 1), out_spaces=[HBM, VMEM],
+        scratch=buffers(owned) + [pltpu.VMEM((owned, width), bf16)] + sems(owned),
+    )
+    new_hot_table, new_hot_state, new_relation_table, new_relation_state = call(
+        shared_step_kernel, "shared_step",
+        [
+            shape((hot, width), f32), shape((hot // LANES, LANES), f32),
+            shape((relation_count, width), f32), shape((relation_count // LANES, LANES), f32),
         ],
-        in_specs=[
-            full(*shared.shape), step_rows, full(hot_rows, LANES), full(relation_count, width), full(relation_rows, LANES),
-        ],
-        out_specs=[step_rows, full(hot_rows, LANES), full(relation_count, width), full(relation_rows, LANES)],
-        scratch_shapes=[pltpu.VMEM((hot, width), f32)],
-        compiler_params=pltpu.CompilerParams(vmem_limit_bytes=20 * 2**20),
-        name="shared_step",
-    )(shared, hot_table, hot_state.reshape(-1, LANES), relation_table, relation_state.reshape(-1, LANES))
-    new_cold_table, new_cold_state = pl.pallas_call(
-        cold_step_kernel,
-        grid=(cold_rows,),
-        out_shape=[shape((owned, width), f32), shape((cold_rows, LANES), f32)],
-        in_specs=[step_rows, step_rows, full(cold_rows, LANES)],
-        out_specs=[step_rows, full(cold_rows, LANES)],
-        compiler_params=pltpu.CompilerParams(vmem_limit_bytes=12 * 2**20),
-        name="cold_step",
-    )(cold_total, cold_table, cold_state.reshape(-1, LANES))
+        (core_at, mine, other, hot_table, state(hot_state), relation_table, state(relation_state)), 61,
+        in_spaces=[SMEM, VMEM, VMEM, HBM, VMEM, HBM, VMEM], out_spaces=[HBM, VMEM, HBM, VMEM],
+        scratch=buffers(hot) + [pltpu.VMEM((hot, width), f32)] + buffers(relation_count)
+        + [pltpu.VMEM((relation_count, width), f32)] + sems(hot + relation_count),
+    )
     return (
         new_hot_table, new_hot_state.reshape(-1), new_cold_table, new_cold_state.reshape(-1),
         new_relation_table, new_relation_state.reshape(-1), mean_loss[0, 0],

time: 244 us -> 228 us (0.934)
  blocking collectives: 47.1 us -> 0 us
  starting transfers between devices: 28.4 us -> 74.3 us
  between operations: 14.4 us -> 1.2 us
  local copies, waits for them, and re-layouts: 23.9 us -> 15.3 us
  Pallas kernels: 59.8 us -> 63.9 us
    all_to_all x2 -> x0, blocking collectives: 47.1 us -> none  [exchange(): lax.all_to_all(array, axis, split_axis=0, concat_axis=0, tiled=True, axis...]
    ppermute x0 -> x15, waiting for transfers between devices: none -> 41.3 us  [the longest x7 27 us: per_device(): sent = {k: lax.ppermute(cold_piece, 'group', way) for k, way in ways}]
    all_gather x1 -> x0, waiting for transfers between devices: 37.8 us -> none  [per_device(): cold_total = lax.all_gather(cold_piece, 'group', axis=0, tiled=True)]
    ppermute x0 -> x15, starting transfers between devices: none -> 35.1 us  [the longest x7 19.9 us: per_device(): lax.ppermute(pieces[k], 'group', way)]
    pallas_call x7 -> x13, Pallas kernels: 52.3 us -> 63.9 us  [call(): pl.pallas_call(kernel, out_shape=out_shape, in_specs=in_spaces or [VMEM]...]
    all_to_all x4 -> x6, starting transfers between devices: 28.2 us -> 39.1 us  [exchange(): lax.all_to_all(array, axis, split_axis=0, concat_axis=0, tiled=True, axis...]
    unnamed x61 -> x54, local copies, waits for them, and re-layouts: 21.5 us -> 13.1 us
    pallas_call x2 -> x0, Pallas kernels: 7.46 us -> none  [the longest x1 5.28 us: per_device(): pl.pallas_call(shared_step_kernel, grid=(hot_rows,), out_shape=[shape((ho...]
  transfers between devices with their start and end apart: 7 -> 22, of which waited for: 5 -> 15; matrix products, arithmetic and copies ran while one was open for 3% -> 4% of each run, Pallas kernels for 7% -> 9%
where the time goes in v3:
time: 228 us; the launch traced here: 225 us
  starting transfers between devices  74.3 us (33%)
  waiting for transfers between devices  64.3 us (28%)
  Pallas kernels  63.9 us (28%)
  local copies, waits for them, and re-layouts  15.3 us (7%)
  other arithmetic  5.85 us (3%)
    pallas_call x13, Pallas kernels, call(): pl.pallas_call(kernel, out_shape=out_shape, in_specs=in_spaces or [VMEM]...  63.9 us
    all_to_all x6, starting transfers between devices, exchange(): lax.all_to_all(array, axis, split_axis=0, concat_axis=0, tiled=True, axis...  39.1 us
    ppermute x7, waiting for transfers between devices, per_device(): sent = {k: lax.ppermute(cold_piece, 'group', way) for k, way in ways}  27 us
    all_to_all x6, waiting for transfers between devices, exchange(): lax.all_to_all(array, axis, split_axis=0, concat_axis=0, tiled=True, axis...  21.5 us
    ppermute x7, starting transfers between devices, per_device(): lax.ppermute(pieces[k], 'group', way)  19.9 us
    ppermute x7, starting transfers between devices, per_device(): sent = {k: lax.ppermute(cold_piece, 'group', way) for k, way in ways}  15.1 us
    ppermute x7, waiting for transfers between devices, per_device(): lax.ppermute(pieces[k], 'group', way)  14.3 us
    unnamed x54, local copies, waits for them, and re-layouts  13.1 us
  transfers between devices with their start and end apart: 22, of which 15 were waited for; matrix products, arithmetic and copies ran while one was open for 4% of the time, Pallas kernels for 9%

profile of v3, /device:TPU:2, one launch (start us, length us, event | category | flops | bytes accessed | tf_op | source)
XLA Modules:
  0.0 224.9 jit_solution(18414310026157010489)
XLA Ops:
  0.6 1.4 requests.1
  2.0 7.6 %all-to-all-start = ((s32[32,1,32]{2,1,0:T(1,128)}), s32[32,1,32]{2,1,0:T(1,128)S(1)}, u32[]{:S(2)}, u32[]{:S(2)}) async-start(s32[32,1,32]{2,1,0:T(1,128)} %requests.1), calls=%async_computation | async-start | bytes 32768 | tf_op jit(solution)/shard_map/all_to_all | solution.py:338
  9.6 2.7 %convert_element_type.9.half_ref = bf16[512,1024]{1,0:T(8,128)(2,1)} convert(f32[512,1024]{1,0:T(8,128)} %table_hbm.1) | non-fusion elementwise | flops 524288 | bytes 3145728 | tf_op jit(solution)/shard_map/convert_element_type | solution.py:362
  12.4 3.4 %all-to-all-done.received_ref = s32[32,1,32]{2,1,0:T(1,128)S(1)} async-done(((s32[32,1,32]{2,1,0:T(1,128)}), s32[32,1,32]{2,1,0:T(1,128)S(1)}, u32[]{:S(2)}, u32[]{:S(2)}) %all-to-all-start) | async-done | bytes 4128 | tf_op jit(solution)/shard_map/all_to_all | solution.py:338
  16.3 3.5 %serve.1 = bf16[1024,1024]{1,0:T(8,128)(2,1)} custom-call(s32[32,1,32]{2,1,0:T(1,128)} %copy-done.21, bf16[512,1024]{1,0:T(8,128)(2,1)} %convert_element_type.9.half_ref), custom_call_target="tpu_custom_call" | custom-call | flops 1073741824 | tf_op jit(solution)/shard_map/serve/pallas_call | solution.py:324
  19.9 5.8 %all-to-all-start.1 = ((bf16[32,32,1024]{2,1,0:T(8,128)(2,1)}), bf16[32,32,1024]{2,1,0:T(8,128)(2,1)}, u32[]{:S(2)}, u32[]{:S(2)}) async-start(bf16[32,32,1024]{2,1,0:T(8,128)(2,1)} %bitcast.26), calls=%async_computation.1 | async-start | bytes 4194304 | tf_op jit(solution)/shard_map/all_to_all | solution.py:338
  25.8 2.2 convert_element_type.10.hot_ref
  29.3 5.3 %early.1 = (bf16[1024,1024]{1,0:T(8,128)(2,1)S(1)}, bf16[1024,1024]{1,0:T(8,128)(2,1)S(1)}, bf16[512,1024]{1,0:T(8,128)(2,1)S(1)}, bf16[1024,1024]{1,0:T(8,128)(2,1)S(1)}) custom-call(bf16[768,1024]{1,0:T(8,128)(2,1)S(1)} %convert_element_type.10.hot_ref, bf16[128,1024]{1,0:T(8,128)(2,1)S(1)} %convert_element_type.11.relation_ref, ...), custom_call_target="tpu_custom_call" | custom-call | flops 4026531840 | tf_op jit(solution)/shard_map/early/pallas_call | solution.py:324
  34.6 1.3 copy-done.13
  35.9 1.4 copy-done.14
  37.3 1.3 copy-done.15
  39.6 12.1 %all-to-all-done.1 = bf16[32,32,1024]{2,1,0:T(8,128)(2,1)} async-done(((bf16[32,32,1024]{2,1,0:T(8,128)(2,1)}), bf16[32,32,1024]{2,1,0:T(8,128)(2,1)}, u32[]{:S(2)}, u32[]{:S(2)}) %all-to-all-start.1) | async-done | bytes 2097184 | tf_op jit(solution)/shard_map/all_to_all | solution.py:338
  51.7 30.5 %block.1 = (bf16[1024,1024]{1,0:T(8,128)(2,1)}, bf16[2560,1024]{1,0:T(8,128)(2,1)}, bf16[1024,1024]{1,0:T(8,128)(2,1)}, f32[8,128]{1,0:T(8,128)}) custom-call(bf16[1024,1024]{1,0:T(8,128)(2,1)} %bitcast.3.cold_hbm, bf16[1024,1024]{1,0:T(8,128)(2,1)} %copy-done.13, bf16[1024,1024]{1,0:T(8,128)(2,1)} %copy-done.14, bf16[512,1024]{1,0:T(8,128)(2,1)} %copy-done.17, ...), custom_call_target="tpu_custom_call" | custom-call | flops 13958643712 | tf_op jit(solution)/shard_map/block/pallas_call | solution.py:324
  82.2 7.2 %all-to-all-start.2 = ((bf16[32,32,1024]{2,1,0:T(8,128)(2,1)}), bf16[32,32,1024]{2,1,0:T(8,128)(2,1)S(1)}, u32[]{:S(2)}, u32[]{:S(2)}) async-start(bf16[32,32,1024]{2,1,0:T(8,128)(2,1)} %bitcast.27), calls=%async_computation.2 | async-start | bytes 4194304 | tf_op jit(solution)/shard_map/all_to_all | solution.py:338
  89.6 2.5 %copy-done.16 = bf16[2560,1024]{1,0:T(8,128)(2,1)S(1)} copy-done((bf16[2560,1024]{1,0:T(8,128)(2,1)S(1)}, bf16[2560,1024]{1,0:T(8,128)(2,1)}, u32[]{:S(2)}) %copy-start.16) | copy-done | bytes 5242904
  92.1 1.6 copy-done.18
  93.7 8.7 %shared.1 = (f32[512,1024]{1,0:T(8,128)S(1)}, bf16[512,1024]{1,0:T(8,128)(2,1)}) custom-call(bf16[2560,1024]{1,0:T(8,128)(2,1)S(1)} %copy-done.16, bf16[1024,1024]{1,0:T(8,128)(2,1)S(1)} %copy-done.18, s32[1,2560]{1,0:T(1,128)S(1)} %compare_select_fusion.places_ref, s32[1,1024]{1,0:T(1,128)S(1)} %bitcast.25, f32[8,128]{1,0:T(8,128)S(1)} %copy-done.19), custom_call_target="tpu_custom_call" | custom-call | flops 7516192768 | tf_op jit(solution)/shard_map/shared/pallas_call | solution.py:324
  102.4 1.3 copy-done.1
  105.2 1.4 collective-permute-done.other_ref
  106.6 1.6 copy-done.2
  109.3 6.0 %all-to-all-done.2 = bf16[32,32,1024]{2,1,0:T(8,128)(2,1)S(1)} async-done(((bf16[32,32,1024]{2,1,0:T(8,128)(2,1)}), bf16[32,32,1024]{2,1,0:T(8,128)(2,1)S(1)}, u32[]{:S(2)}, u32[]{:S(2)}) %all-to-all-start.2) | async-done | bytes 2097184 | tf_op jit(solution)/shard_map/all_to_all | solution.py:338
  116.6 6.7 %all-to-all-start.3 = ((bf16[16,32,1024]{2,1,0:T(8,128)(2,1)}), bf16[16,32,1024]{2,1,0:T(8,128)(2,1)S(1)}, u32[]{:S(2)}, u32[]{:S(2)}) async-start(bf16[16,32,1024]{2,1,0:T(8,128)(2,1)} %bitcast.13), calls=%async_computation.3 | async-start | bytes 2097152 | tf_op jit(solution)/shard_map/all_to_all | solution.py:338
  123.3 1.9 collective-permute-start.1
  125.3 3.3 %collective-permute-start.2 = (bf16[64,1024]{1,0:T(8,128)(2,1)S(1)}, bf16[64,1024]{1,0:T(8,128)(2,1)S(1)}, u32[]{:S(2)}, u32[]{:S(2)}) collective-permute-start(bf16[64,1024]{1,0:T(8,128)(2,1)S(1)} %get-tuple-element.47), channel_id=1, source_target_pairs={{0,64},{32,96},{64,128},{96,160},{128,192},{160,224},{192,0},{224,... | collective-permute-start | bytes 393224 | tf_op jit(solution)/shard_map/ppermute | solution.py:418
  128.5 4.1 %collective-permute-start.3 = (bf16[64,1024]{1,0:T(8,128)(2,1)S(1)}, bf16[64,1024]{1,0:T(8,128)(2,1)S(1)}, u32[]{:S(2)}, u32[]{:S(2)}) collective-permute-start(bf16[64,1024]{1,0:T(8,128)(2,1)S(1)} %get-tuple-element.48), channel_id=1, source_target_pairs={{0,96},{32,128},{64,160},{96,192},{128,224},{160,0},{192,32},{224,... | collective-permute-start | bytes 393224 | tf_op jit(solution)/shard_map/ppermute | solution.py:418
  133.1 4.9 %collective-permute-start.5 = (bf16[64,1024]{1,0:T(8,128)(2,1)S(1)}, bf16[64,1024]{1,0:T(8,128)(2,1)S(1)}, u32[]{:S(2)}, u32[]{:S(2)}) collective-permute-start(bf16[64,1024]{1,0:T(8,128)(2,1)S(1)} %get-tuple-element.50), channel_id=1, source_target_pairs={{0,160},{32,192},{64,224},{96,0},{128,32},{160,64},{192,96},{224,1... | collective-permute-start | bytes 393224 | tf_op jit(solution)/shard_map/ppermute | solution.py:418
  138.1 2.7 %collective-permute-start.6 = (bf16[64,1024]{1,0:T(8,128)(2,1)S(1)}, bf16[64,1024]{1,0:T(8,128)(2,1)S(1)}, u32[]{:S(2)}, u32[]{:S(2)}) collective-permute-start(bf16[64,1024]{1,0:T(8,128)(2,1)S(1)} %get-tuple-element.51), channel_id=1, source_target_pairs={{0,192},{32,224},{64,0},{96,32},{128,64},{160,96},{192,128},{224,1... | collective-permute-start | bytes 393224 | tf_op jit(solution)/shard_map/ppermute | solution.py:418
  140.7 3.1 %collective-permute-done.2.refs_2_ = bf16[64,1024]{1,0:T(8,128)(2,1)S(1)} collective-permute-done((bf16[64,1024]{1,0:T(8,128)(2,1)S(1)}, bf16[64,1024]{1,0:T(8,128)(2,1)S(1)}, u32[]{:S(2)}, u32[]{:S(2)}) %collective-permute-start.2) | collective-permute-done | bytes 131104 | tf_op jit(solution)/shard_map/ppermute | solution.py:418
  143.8 2.6 %collective-permute-start.7 = (bf16[64,1024]{1,0:T(8,128)(2,1)S(1)}, bf16[64,1024]{1,0:T(8,128)(2,1)S(1)}, u32[]{:S(2)}, u32[]{:S(2)}) collective-permute-start(bf16[64,1024]{1,0:T(8,128)(2,1)S(1)} %get-tuple-element.52), channel_id=1, source_target_pairs={{0,224},{32,0},{64,32},{96,64},{128,96},{160,128},{192,160},{224,1... | collective-permute-start | bytes 393224 | tf_op jit(solution)/shard_map/ppermute | solution.py:418
  146.4 3.7 %collective-permute-done.3.refs_3_ = bf16[64,1024]{1,0:T(8,128)(2,1)S(1)} collective-permute-done((bf16[64,1024]{1,0:T(8,128)(2,1)S(1)}, bf16[64,1024]{1,0:T(8,128)(2,1)S(1)}, u32[]{:S(2)}, u32[]{:S(2)}) %collective-permute-start.3) | collective-permute-done | bytes 131104 | tf_op jit(solution)/shard_map/ppermute | solution.py:418
  150.1 3.8 %collective-permute-done.5.refs_5_ = bf16[64,1024]{1,0:T(8,128)(2,1)S(1)} collective-permute-done((bf16[64,1024]{1,0:T(8,128)(2,1)S(1)}, bf16[64,1024]{1,0:T(8,128)(2,1)S(1)}, u32[]{:S(2)}, u32[]{:S(2)}) %collective-permute-start.5) | collective-permute-done | bytes 131104 | tf_op jit(solution)/shard_map/ppermute | solution.py:418
  153.9 1.9 collective-permute-done.6.refs_6_
  155.8 1.8 collective-permute-done.7.refs_7_
  158.8 4.5 %all-to-all-start.4 = ((bf16[8,32,1024]{2,1,0:T(8,128)(2,1)}), bf16[8,32,1024]{2,1,0:T(8,128)(2,1)S(1)}, u32[]{:S(2)}, u32[]{:S(2)}) async-start(bf16[8,32,1024]{2,1,0:T(8,128)(2,1)} %member_sum.1), calls=%async_computation.4 | async-start | bytes 1048576 | tf_op jit(solution)/shard_map/all_to_all | solution.py:338
  163.3 2.0 collective-permute-start.8
  166.6 1.7 collective-permute-start.10
  168.2 2.5 %collective-permute-start.11 = (bf16[64,1024]{1,0:T(8,128)(2,1)S(1)}, bf16[64,1024]{1,0:T(8,128)(2,1)S(1)}, u32[]{:S(2)}, u32[]{:S(2)}) collective-permute-start(bf16[64,1024]{1,0:T(8,128)(2,1)S(1)} %cold_sum.1._after.refs_0_), channel_id=1, source_target_pairs={{0,192},{32,224},{64,0},{96,32},{128,64},{160,96},{192,128},{224,1... | collective-permute-start | bytes 393224 | tf_op jit(solution)/shard_map/ppermute | solution.py:426
  170.7 12.0 %collective-permute-done.8.refs_0_.refs_1_ = bf16[64,1024]{1,0:T(8,128)(2,1)S(1)} collective-permute-done((bf16[64,1024]{1,0:T(8,128)(2,1)S(1)}, bf16[64,1024]{1,0:T(8,128)(2,1)S(1)}, u32[]{:S(2)}, u32[]{:S(2)}) %collective-permute-start.8) | collective-permute-done | bytes 131104 | tf_op jit(solution)/shard_map/ppermute | solution.py:426
  182.7 3.4 %collective-permute-done.10.refs_2_ = bf16[64,1024]{1,0:T(8,128)(2,1)S(1)} collective-permute-done((bf16[64,1024]{1,0:T(8,128)(2,1)S(1)}, bf16[64,1024]{1,0:T(8,128)(2,1)S(1)}, u32[]{:S(2)}, u32[]{:S(2)}) %collective-permute-start.10) | collective-permute-done | bytes 131104 | tf_op jit(solution)/shard_map/ppermute | solution.py:426
  187.4 7.3 %all-to-all-start.5 = ((bf16[16,32,1024]{2,1,0:T(8,128)(2,1)}), bf16[16,32,1024]{2,1,0:T(8,128)(2,1)S(1)}, u32[]{:S(2)}, u32[]{:S(2)}) async-start(bf16[16,32,1024]{2,1,0:T(8,128)(2,1)} %get-tuple-element.53), calls=%async_computation.5 | async-start | bytes 2097152 | tf_op jit(solution)/shard_map/all_to_all | solution.py:338
  194.6 3.6 %collective-permute-start.12 = (bf16[64,1024]{1,0:T(8,128)(2,1)S(1)}, bf16[64,1024]{1,0:T(8,128)(2,1)S(1)}, u32[]{:S(2)}, u32[]{:S(2)}) collective-permute-start(bf16[64,1024]{1,0:T(8,128)(2,1)S(1)} %cold_sum.1._after.refs_0_), channel_id=1, source_target_pairs={{0,96},{32,128},{64,160},{96,192},{128,224},{160,0},{192,32},{224,... | collective-permute-start | bytes 393224 | tf_op jit(solution)/shard_map/ppermute | solution.py:426
  198.2 1.5 collective-permute-start.13
  199.7 2.6 %collective-permute-start.14 = (bf16[64,1024]{1,0:T(8,128)(2,1)S(1)}, bf16[64,1024]{1,0:T(8,128)(2,1)S(1)}, u32[]{:S(2)}, u32[]{:S(2)}) collective-permute-start(bf16[64,1024]{1,0:T(8,128)(2,1)S(1)} %cold_sum.1._after.refs_0_), channel_id=1, source_target_pairs={{0,128},{32,160},{64,192},{96,224},{128,0},{160,32},{192,64},{224,... | collective-permute-start | bytes 393224 | tf_op jit(solution)/shard_map/ppermute | solution.py:426
  202.3 5.3 %collective-permute-done.12.refs_1_.refs_3_ = bf16[64,1024]{1,0:T(8,128)(2,1)S(1)} collective-permute-done((bf16[64,1024]{1,0:T(8,128)(2,1)S(1)}, bf16[64,1024]{1,0:T(8,128)(2,1)S(1)}, u32[]{:S(2)}, u32[]{:S(2)}) %collective-permute-start.12) | collective-permute-done | bytes 131104 | tf_op jit(solution)/shard_map/ppermute | solution.py:426
  207.6 2.4 %collective-permute-done.13.refs_2_.refs_5_ = bf16[64,1024]{1,0:T(8,128)(2,1)S(1)} collective-permute-done((bf16[64,1024]{1,0:T(8,128)(2,1)S(1)}, bf16[64,1024]{1,0:T(8,128)(2,1)S(1)}, u32[]{:S(2)}, u32[]{:S(2)}) %collective-permute-start.13) | collective-permute-done | bytes 131104 | tf_op jit(solution)/shard_map/ppermute | solution.py:426
  210.0 3.7 %collective-permute-done.14.refs_3_.refs_4_ = bf16[64,1024]{1,0:T(8,128)(2,1)S(1)} collective-permute-done((bf16[64,1024]{1,0:T(8,128)(2,1)S(1)}, bf16[64,1024]{1,0:T(8,128)(2,1)S(1)}, u32[]{:S(2)}, u32[]{:S(2)}) %collective-permute-start.14) | collective-permute-done | bytes 131104 | tf_op jit(solution)/shard_map/ppermute | solution.py:426
  214.4 4.5 %cold_step.1 = (f32[512,1024]{1,0:T(8,128)}, f32[4,128]{1,0:T(4,128)}) custom-call(s32[1]{0:T(128)} %bitcast.1.group_ref, f32[512,1024]{1,0:T(8,128)} %table_hbm.1, f32[4,128]{1,0:T(4,128)} %bitcast.36, bf16[64,1024]{1,0:T(8,128)(2,1)} %copy-done.3, bf16[64,1024]{1,0:T(8,128)(2,1)} %copy-done.8, bf16[64,1024]{1,0:T(8,128)(2,1)} %copy-done.10, ...), custom_call_target="tpu_custom_call" | custom-call | tf_op jit(solution)/shard_map/cold_step/pallas_call | solution.py:324
  219.4 5.3 %shared_step.1 = (f32[768,1024]{1,0:T(8,128)}, f32[6,128]{1,0:T(8,128)}, f32[128,1024]{1,0:T(8,128)}, f32[1,128]{1,0:T(1,128)}) custom-call(s32[1]{0:T(128)} %bitcast.core_ref, bf16[512,1024]{1,0:T(8,128)(2,1)} %copy-done, bf16[512,1024]{1,0:T(8,128)(2,1)} %collective-permute-done.15.other_ref, f32[768,1024]{1,0:T(8,128)} %hot_hbm.1, f32[6,128]{1,0:T(8,128)} %bitcast.35, ...), custom_call_target="tpu_custom_call" | custom-call | tf_op jit(solution)/shard_map/shared_step/pallas_call | solution.py:324
  (77 shorter events, 12.2 us)
Async XLA Ops:
  2.0 13.7 %all-to-all-start = ((s32[32,1,32]{2,1,0:T(1,128)}), s32[32,1,32]{2,1,0:T(1,128)S(1)}, u32[]{:S(2)}, u32[]{:S(2)}) async-start(s32[32,1,32]{2,1,0:T(1,128)} %requests.1), calls=%async_computation | async-start | bytes 32768 | tf_op jit(solution)/shard_map/all_to_all | solution.py:338
  19.9 31.8 %all-to-all-start.1 = ((bf16[32,32,1024]{2,1,0:T(8,128)(2,1)}), bf16[32,32,1024]{2,1,0:T(8,128)(2,1)}, u32[]{:S(2)}, u32[]{:S(2)}) async-start(bf16[32,32,1024]{2,1,0:T(8,128)(2,1)} %bitcast.26), calls=%async_computation.1 | async-start | bytes 4194304 | tf_op jit(solution)/shard_map/all_to_all | solution.py:338
  25.7 2.2 %copy-start.20 = (f32[128,1024]{1,0:T(8,128)S(1)}, f32[128,1024]{1,0:T(8,128)}, u32[]{:S(2)}) copy-start(f32[128,1024]{1,0:T(8,128)} %relation_hbm.1) | copy-start | bytes 1572868
  25.7 2.3 %copy-start.23 = (s32[1024]{0:T(1024)S(1)}, s32[1024]{0:T(1024)}, u32[]{:S(2)}) copy-start(s32[1024]{0:T(1024)} %param.20) | copy-start | bytes 12292
  25.7 2.3 %copy-start.24 = (s32[1024]{0:T(1024)S(1)}, s32[1024]{0:T(1024)}, u32[]{:S(2)}) copy-start(s32[1024]{0:T(1024)} %param.18) | copy-start | bytes 12292
  25.8 2.3 %copy-start.26 = (s32[1024]{0:T(1024)S(1)}, s32[1024]{0:T(1024)}, u32[]{:S(2)}) copy-start(s32[1024]{0:T(1024)} %param.19) | copy-start | bytes 12292
  25.8 2.5 %copy-start.25 = (s32[1,512]{1,0:T(1,128)S(1)}, s32[1,512]{1,0:T(1,128)}, u32[]{:S(2)}) copy-start(s32[1,512]{1,0:T(1,128)} %param.21) | copy-start | bytes 6148
  28.3 6.3 %copy-start.7 = (s32[1024,4]{1,0:T(8,128)}, s32[1024,4]{1,0:T(8,128)S(1)}, u32[]{:S(2)}) copy-start(s32[1024,4]{1,0:T(8,128)S(1)} %copy.22.columns_ref.columns_hbm) | copy-start | bytes 49156
  28.5 6.1 %copy-start.12 = (s32[512,1]{1,0:T(8,128)}, s32[512,1]{1,0:T(8,128)S(1)}, u32[]{:S(2)}) copy-start(s32[512,1]{1,0:T(8,128)S(1)} %copy.23.negative_column_ref.negative_column_hbm) | copy-start | bytes 6148
  34.6 1.3 copy-start.13
  35.9 1.4 copy-start.14
  37.3 1.3 copy-start.15
  38.6 1.0 copy-start.17
  82.2 7.4 %copy-start.19 = (f32[8,128]{1,0:T(8,128)S(1)}, f32[8,128]{1,0:T(8,128)}, u32[]{:S(2)}) copy-start(f32[8,128]{1,0:T(8,128)} %get-tuple-element.41.loss_ref) | copy-start | bytes 12292
  82.2 33.1 %all-to-all-start.2 = ((bf16[32,32,1024]{2,1,0:T(8,128)(2,1)}), bf16[32,32,1024]{2,1,0:T(8,128)(2,1)S(1)}, u32[]{:S(2)}, u32[]{:S(2)}) async-start(bf16[32,32,1024]{2,1,0:T(8,128)(2,1)} %bitcast.27), calls=%async_computation.2 | async-start | bytes 4194304 | tf_op jit(solution)/shard_map/all_to_all | solution.py:338
  89.6 2.5 %copy-start.16 = (bf16[2560,1024]{1,0:T(8,128)(2,1)S(1)}, bf16[2560,1024]{1,0:T(8,128)(2,1)}, u32[]{:S(2)}) copy-start(bf16[2560,1024]{1,0:T(8,128)(2,1)} %get-tuple-element.39.grads_ref) | copy-start | bytes 15728644
  92.1 1.6 copy-start.18
  93.7 10.7 %copy-start.22 = (s32[32,1,32]{2,1,0:T(1,128)S(1)}, s32[32,1,32]{2,1,0:T(1,128)}, u32[]{:S(2)}) copy-start(s32[32,1,32]{2,1,0:T(1,128)} %copy-done.21) | copy-start | bytes 12292
  102.4 1.3 copy-start.1
  103.7 2.9 %collective-permute-start = (bf16[512,1024]{1,0:T(8,128)(2,1)}, bf16[512,1024]{1,0:T(8,128)(2,1)S(1)}, u32[]{:S(2)}, u32[]{:S(2)}) collective-permute-start(bf16[512,1024]{1,0:T(8,128)(2,1)} %get-tuple-element.43), channel_id=1, source_target_pairs={{0,1},{1,0},{2,3},{3,2},{4,5},{5,4},{6,7},{7,6},{8,9},{9,8},{10,11... | collective-permute-start | bytes 3145736 | tf_op jit(solution)/shard_map/ppermute | solution.py:409
  106.6 1.6 copy-start.2
  116.6 41.2 %all-to-all-start.3 = ((bf16[16,32,1024]{2,1,0:T(8,128)(2,1)}), bf16[16,32,1024]{2,1,0:T(8,128)(2,1)S(1)}, u32[]{:S(2)}, u32[]{:S(2)}) async-start(bf16[16,32,1024]{2,1,0:T(8,128)(2,1)} %bitcast.13), calls=%async_computation.3 | async-start | bytes 2097152 | tf_op jit(solution)/shard_map/all_to_all | solution.py:338
  123.3 14.7 %collective-permute-start.1 = (bf16[64,1024]{1,0:T(8,128)(2,1)S(1)}, bf16[64,1024]{1,0:T(8,128)(2,1)S(1)}, u32[]{:S(2)}, u32[]{:S(2)}) collective-permute-start(bf16[64,1024]{1,0:T(8,128)(2,1)S(1)} %get-tuple-element.46), channel_id=1, source_target_pairs={{0,32},{32,64},{64,96},{96,128},{128,160},{160,192},{192,224},{224... | collective-permute-start | bytes 393224 | tf_op jit(solution)/shard_map/ppermute | solution.py:418
  125.3 18.6 %collective-permute-start.2 = (bf16[64,1024]{1,0:T(8,128)(2,1)S(1)}, bf16[64,1024]{1,0:T(8,128)(2,1)S(1)}, u32[]{:S(2)}, u32[]{:S(2)}) collective-permute-start(bf16[64,1024]{1,0:T(8,128)(2,1)S(1)} %get-tuple-element.47), channel_id=1, source_target_pairs={{0,64},{32,96},{64,128},{96,160},{128,192},{160,224},{192,0},{224,... | collective-permute-start | bytes 393224 | tf_op jit(solution)/shard_map/ppermute | solution.py:418
  128.5 21.5 %collective-permute-start.3 = (bf16[64,1024]{1,0:T(8,128)(2,1)S(1)}, bf16[64,1024]{1,0:T(8,128)(2,1)S(1)}, u32[]{:S(2)}, u32[]{:S(2)}) collective-permute-start(bf16[64,1024]{1,0:T(8,128)(2,1)S(1)} %get-tuple-element.48), channel_id=1, source_target_pairs={{0,96},{32,128},{64,160},{96,192},{128,224},{160,0},{192,32},{224,... | collective-permute-start | bytes 393224 | tf_op jit(solution)/shard_map/ppermute | solution.py:418
  132.6 17.5 %collective-permute-start.4 = (bf16[64,1024]{1,0:T(8,128)(2,1)S(1)}, bf16[64,1024]{1,0:T(8,128)(2,1)S(1)}, u32[]{:S(2)}, u32[]{:S(2)}) collective-permute-start(bf16[64,1024]{1,0:T(8,128)(2,1)S(1)} %get-tuple-element.49), channel_id=1, source_target_pairs={{0,128},{32,160},{64,192},{96,224},{128,0},{160,32},{192,64},{224,... | collective-permute-start | bytes 393224 | tf_op jit(solution)/shard_map/ppermute | solution.py:418
  133.1 20.8 %collective-permute-start.5 = (bf16[64,1024]{1,0:T(8,128)(2,1)S(1)}, bf16[64,1024]{1,0:T(8,128)(2,1)S(1)}, u32[]{:S(2)}, u32[]{:S(2)}) collective-permute-start(bf16[64,1024]{1,0:T(8,128)(2,1)S(1)} %get-tuple-element.50), channel_id=1, source_target_pairs={{0,160},{32,192},{64,224},{96,0},{128,32},{160,64},{192,96},{224,1... | collective-permute-start | bytes 393224 | tf_op jit(solution)/shard_map/ppermute | solution.py:418
  138.1 17.8 %collective-permute-start.6 = (bf16[64,1024]{1,0:T(8,128)(2,1)S(1)}, bf16[64,1024]{1,0:T(8,128)(2,1)S(1)}, u32[]{:S(2)}, u32[]{:S(2)}) collective-permute-start(bf16[64,1024]{1,0:T(8,128)(2,1)S(1)} %get-tuple-element.51), channel_id=1, source_target_pairs={{0,192},{32,224},{64,0},{96,32},{128,64},{160,96},{192,128},{224,1... | collective-permute-start | bytes 393224 | tf_op jit(solution)/shard_map/ppermute | solution.py:418
  143.8 13.8 %collective-permute-start.7 = (bf16[64,1024]{1,0:T(8,128)(2,1)S(1)}, bf16[64,1024]{1,0:T(8,128)(2,1)S(1)}, u32[]{:S(2)}, u32[]{:S(2)}) collective-permute-start(bf16[64,1024]{1,0:T(8,128)(2,1)S(1)} %get-tuple-element.52), channel_id=1, source_target_pairs={{0,224},{32,0},{64,32},{96,64},{128,96},{160,128},{192,160},{224,1... | collective-permute-start | bytes 393224 | tf_op jit(solution)/shard_map/ppermute | solution.py:418
  157.8 41.9 %copy-start.3 = (bf16[64,1024]{1,0:T(8,128)(2,1)}, bf16[64,1024]{1,0:T(8,128)(2,1)S(1)}, u32[]{:S(2)}) copy-start(bf16[64,1024]{1,0:T(8,128)(2,1)S(1)} %cold_sum.1._after.refs_0_) | copy-start | bytes 393220
  158.8 27.4 %all-to-all-start.4 = ((bf16[8,32,1024]{2,1,0:T(8,128)(2,1)}), bf16[8,32,1024]{2,1,0:T(8,128)(2,1)S(1)}, u32[]{:S(2)}, u32[]{:S(2)}) async-start(bf16[8,32,1024]{2,1,0:T(8,128)(2,1)} %member_sum.1), calls=%async_computation.4 | async-start | bytes 1048576 | tf_op jit(solution)/shard_map/all_to_all | solution.py:338
  163.3 19.4 %collective-permute-start.8 = (bf16[64,1024]{1,0:T(8,128)(2,1)S(1)}, bf16[64,1024]{1,0:T(8,128)(2,1)S(1)}, u32[]{:S(2)}, u32[]{:S(2)}) collective-permute-start(bf16[64,1024]{1,0:T(8,128)(2,1)S(1)} %cold_sum.1._after.refs_0_), channel_id=1, source_target_pairs={{0,32},{32,64},{64,96},{96,128},{128,160},{160,192},{192,224},{224... | collective-permute-start | bytes 393224 | tf_op jit(solution)/shard_map/ppermute | solution.py:426
  165.3 17.3 %collective-permute-start.9 = (bf16[64,1024]{1,0:T(8,128)(2,1)S(1)}, bf16[64,1024]{1,0:T(8,128)(2,1)S(1)}, u32[]{:S(2)}, u32[]{:S(2)}) collective-permute-start(bf16[64,1024]{1,0:T(8,128)(2,1)S(1)} %cold_sum.1._after.refs_0_), channel_id=1, source_target_pairs={{0,224},{32,0},{64,32},{96,64},{128,96},{160,128},{192,160},{224,1... | collective-permute-start | bytes 393224 | tf_op jit(solution)/shard_map/ppermute | solution.py:426
  166.6 19.5 %collective-permute-start.10 = (bf16[64,1024]{1,0:T(8,128)(2,1)S(1)}, bf16[64,1024]{1,0:T(8,128)(2,1)S(1)}, u32[]{:S(2)}, u32[]{:S(2)}) collective-permute-start(bf16[64,1024]{1,0:T(8,128)(2,1)S(1)} %cold_sum.1._after.refs_0_), channel_id=1, source_target_pairs={{0,64},{32,96},{64,128},{96,160},{128,192},{160,224},{192,0},{224,... | collective-permute-start | bytes 393224 | tf_op jit(solution)/shard_map/ppermute | solution.py:426
  168.2 18.0 %collective-permute-start.11 = (bf16[64,1024]{1,0:T(8,128)(2,1)S(1)}, bf16[64,1024]{1,0:T(8,128)(2,1)S(1)}, u32[]{:S(2)}, u32[]{:S(2)}) collective-permute-start(bf16[64,1024]{1,0:T(8,128)(2,1)S(1)} %cold_sum.1._after.refs_0_), channel_id=1, source_target_pairs={{0,192},{32,224},{64,0},{96,32},{128,64},{160,96},{192,128},{224,1... | collective-permute-start | bytes 393224 | tf_op jit(solution)/shard_map/ppermute | solution.py:426
  182.7 31.1 %copy-start.8 = (bf16[64,1024]{1,0:T(8,128)(2,1)}, bf16[64,1024]{1,0:T(8,128)(2,1)S(1)}, u32[]{:S(2)}) copy-start(bf16[64,1024]{1,0:T(8,128)(2,1)S(1)} %collective-permute-done.8.refs_0_.refs_1_) | copy-start | bytes 393220
  182.7 31.1 %copy-start.9 = (bf16[64,1024]{1,0:T(8,128)(2,1)}, bf16[64,1024]{1,0:T(8,128)(2,1)S(1)}, u32[]{:S(2)}) copy-start(bf16[64,1024]{1,0:T(8,128)(2,1)S(1)} %collective-permute-done.9.refs_1_.refs_7_) | copy-start | bytes 393220
  186.1 27.7 %copy-start.10 = (bf16[64,1024]{1,0:T(8,128)(2,1)}, bf16[64,1024]{1,0:T(8,128)(2,1)S(1)}, u32[]{:S(2)}) copy-start(bf16[64,1024]{1,0:T(8,128)(2,1)S(1)} %collective-permute-done.10.refs_2_) | copy-start | bytes 393220
  186.2 27.5 %copy-start.11 = (bf16[64,1024]{1,0:T(8,128)(2,1)}, bf16[64,1024]{1,0:T(8,128)(2,1)S(1)}, u32[]{:S(2)}) copy-start(bf16[64,1024]{1,0:T(8,128)(2,1)S(1)} %collective-permute-done.11.refs_3_.refs_6_) | copy-start | bytes 393220
  187.4 26.4 %all-to-all-start.5 = ((bf16[16,32,1024]{2,1,0:T(8,128)(2,1)}), bf16[16,32,1024]{2,1,0:T(8,128)(2,1)S(1)}, u32[]{:S(2)}, u32[]{:S(2)}) async-start(bf16[16,32,1024]{2,1,0:T(8,128)(2,1)} %get-tuple-element.53), calls=%async_computation.5 | async-start | bytes 2097152 | tf_op jit(solution)/shard_map/all_to_all | solution.py:338
  194.6 13.0 %collective-permute-start.12 = (bf16[64,1024]{1,0:T(8,128)(2,1)S(1)}, bf16[64,1024]{1,0:T(8,128)(2,1)S(1)}, u32[]{:S(2)}, u32[]{:S(2)}) collective-permute-start(bf16[64,1024]{1,0:T(8,128)(2,1)S(1)} %cold_sum.1._after.refs_0_), channel_id=1, source_target_pairs={{0,96},{32,128},{64,160},{96,192},{128,224},{160,0},{192,32},{224,... | collective-permute-start | bytes 393224 | tf_op jit(solution)/shard_map/ppermute | solution.py:426
  198.2 11.8 %collective-permute-start.13 = (bf16[64,1024]{1,0:T(8,128)(2,1)S(1)}, bf16[64,1024]{1,0:T(8,128)(2,1)S(1)}, u32[]{:S(2)}, u32[]{:S(2)}) collective-permute-start(bf16[64,1024]{1,0:T(8,128)(2,1)S(1)} %cold_sum.1._after.refs_0_), channel_id=1, source_target_pairs={{0,160},{32,192},{64,224},{96,0},{128,32},{160,64},{192,96},{224,1... | collective-permute-start | bytes 393224 | tf_op jit(solution)/shard_map/ppermute | solution.py:426
  199.7 14.1 %collective-permute-start.14 = (bf16[64,1024]{1,0:T(8,128)(2,1)S(1)}, bf16[64,1024]{1,0:T(8,128)(2,1)S(1)}, u32[]{:S(2)}, u32[]{:S(2)}) collective-permute-start(bf16[64,1024]{1,0:T(8,128)(2,1)S(1)} %cold_sum.1._after.refs_0_), channel_id=1, source_target_pairs={{0,128},{32,160},{64,192},{96,224},{128,0},{160,32},{192,64},{224,... | collective-permute-start | bytes 393224 | tf_op jit(solution)/shard_map/ppermute | solution.py:426
  207.6 6.2 %copy-start.4 = (bf16[64,1024]{1,0:T(8,128)(2,1)}, bf16[64,1024]{1,0:T(8,128)(2,1)S(1)}, u32[]{:S(2)}) copy-start(bf16[64,1024]{1,0:T(8,128)(2,1)S(1)} %collective-permute-done.12.refs_1_.refs_3_) | copy-start | bytes 393220
  210.0 3.9 %copy-start.5 = (bf16[64,1024]{1,0:T(8,128)(2,1)}, bf16[64,1024]{1,0:T(8,128)(2,1)S(1)}, u32[]{:S(2)}) copy-start(bf16[64,1024]{1,0:T(8,128)(2,1)S(1)} %collective-permute-done.13.refs_2_.refs_5_) | copy-start | bytes 393220
  213.7 0.6 copy-start.6
  213.8 5.6 %copy-start = (bf16[512,1024]{1,0:T(8,128)(2,1)}, bf16[512,1024]{1,0:T(8,128)(2,1)S(1)}, u32[]{:S(2)}) copy-start(bf16[512,1024]{1,0:T(8,128)(2,1)S(1)} %after_far.1.mine_ref) | copy-start | bytes 3145732
  213.8 5.6 %collective-permute-start.15 = (bf16[512,1024]{1,0:T(8,128)(2,1)S(1)}, bf16[512,1024]{1,0:T(8,128)(2,1)}, u32[]{:S(2)}, u32[]{:S(2)}) collective-permute-start(bf16[512,1024]{1,0:T(8,128)(2,1)S(1)} %after_far.1.mine_ref), channel_id=1, source_target_pairs={{0,1},{1,0},{2,3},{3,2},{4,5},{5,4},{6,7},{7,6},{8,9},{9,8},{10,11... | collective-permute-start | bytes 3145736 | tf_op jit(solution)/shard_map/ppermute | solution.py:439
  (1 other events, 0.6 us)
